TPU v7x, 512 devices: a whole 4x8x8 slice. The times are simulated.
512 devices in a mesh: row: 32 (over y, x), col: 16 (over z, core).
Axes of the slice: x: 4, y: 8, z: 8, core: 2. Of those that a mesh axis runs over, the one named last changes fastest.
Arguments:
- density: bfloat16 [384, 32, 128, 128], P('row', 'col'), may hold values from -0.6 to 0.6, as said below
- density_pattern: int32 [384, 32], P('row', 'col'), may hold values from 0 to 1, as said below
- filter_pattern: int32 [384, 32], P('row', 'col'), may hold values from 0 to 1, as said below
Outputs:
- purified: bfloat16 [384, 32, 128, 128], P('row', 'col')
Inputs may be any that keep to these rules, and one draw needn't show every extreme that they name: `density`: the tiles form a symmetric matrix: the tile of block row i at block column j is the transpose of the tile of block row j at block column i, and each diagonal tile is symmetric. `density_pattern`: 1 marks a tile of the pattern. With n = 16, slot s = c * 2 + q of block row i stands for block column (i + d) mod 384, d = -8 + ((c - i + 8) mod n) + q * n; a slot with d > 8 is always 0, the slot with d = 0 is always 1, and the pattern is symmetric: (i, j) is marked exactly when (j, i) is. `filter_pattern`: 1 marks a tile kept in the filtered products, with the slots as for density_pattern; a slot with d > 8 is always 0, the slot with d = 0 is always 1, and the pattern is symmetric.
All inputs are finite; a program needn't handle non-finite values.
Results may differ from a plain program's by a relative error of at most 0.0041.
Values may be sent and summed in bfloat16 or wider, within the bound.
No kernel may reach another device: no remote copies, remote signals or barrier semaphores. Data moves between devices by JAX's collectives and lax.ppermute only.
A program may use at most 128 MiB of HBM per device.

v0:
```python
import math

import jax
import jax.numpy as jnp
from jax import lax
from jax.sharding import PartitionSpec as P

W = 8


def padded(value, sides, width):
    for axis, dim in sides:
        size, length = (lax.axis_size(axis), value.shape[dim])
        up = [(i, (i + 1) % size) for i in range(size)]
        down = [(j, i) for i, j in up]
        last = lax.slice_in_dim(value, length - width, length, axis=dim)
        leading = lax.slice_in_dim(value, 0, width, axis=dim)
        before = lax.ppermute(last, axis, up)
        after = lax.ppermute(leading, axis, down)
        value = jnp.concatenate([before, value, after], axis=dim)
    return value


def per_device(density, density_pattern, filter_pattern):
    rows_dev = density_pattern.shape[0]
    slots_dev = density_pattern.shape[1]
    tile_size = density.shape[2]
    groups = lax.axis_size("col")
    row_index = lax.axis_index("row")
    col_index = lax.axis_index("col")
    zero_tile = jnp.zeros((), density.dtype)
    masked = jnp.where((density_pattern == 1)[:, :, None, None], density, zero_tile)
    local_rows = jnp.arange(rows_dev, dtype=jnp.int32)
    global_rows = row_index * rows_dev + local_rows
    row_table = padded(masked, (("row", 0),), W)
    anchor = local_rows + W
    table_rows = row_table.shape[0]
    table_flat = row_table.reshape(table_rows * slots_dev, tile_size, tile_size)
    residue = jnp.mod(col_index - global_rows + W, groups)
    out_slots = jnp.arange(slots_dev, dtype=jnp.int32)
    block_count = math.gcd(rows_dev, 8)
    block_rows = rows_dev // block_count

    def accumulate(panel_piece):
        piece_width = panel_piece.shape[1]
        slot_ids = jnp.arange(piece_width, dtype=jnp.int32)
        group_ids = slot_ids // slots_dev
        within = slot_ids % slots_dev
        offset = (
            -W
            + jnp.mod(group_ids[None, :] - global_rows[:, None] + W, groups)
            + within[None, :] * groups
        )
        column_slot = out_slots[None, :, None] + jnp.floor_divide(
            residue[:, None, None] - offset[:, None, :], groups
        )
        usable = (offset[:, None, :] <= W) & (column_slot >= 0) & (column_slot < slots_dev)
        position = jnp.mod(anchor[:, None, None] + offset[:, None, :], table_rows)
        flat_index = position * slots_dev + jnp.clip(column_slot, 0, slots_dev - 1)

        def one_block(operands):
            piece_block, index_block, usable_block = operands
            fetched = jnp.take(table_flat, index_block.reshape(-1), axis=0)
            fetched = fetched.reshape(index_block.shape + (tile_size, tile_size))
            fetched = jnp.where(usable_block[..., None, None], fetched, zero_tile)
            return jnp.einsum(
                "itab,iftbc->ifac", piece_block, fetched, preferred_element_type=jnp.float32
            )

        partial_value = lax.map(
            one_block,
            (
                panel_piece.reshape(block_count, block_rows, piece_width, tile_size, tile_size),
                flat_index.reshape(block_count, block_rows, slots_dev, piece_width),
                usable.reshape(block_count, block_rows, slots_dev, piece_width),
            ),
        )
        return partial_value.reshape(rows_dev, slots_dev, tile_size, tile_size)

    keeping = (filter_pattern == 1)[:, :, None, None]
    square_sum = accumulate(lax.all_gather(masked, "col", axis=1, tiled=True))
    square = jnp.where(keeping, square_sum, jnp.zeros((), jnp.float32)).astype(jnp.bfloat16)
    cubic_sum = accumulate(lax.all_gather(square, "col", axis=1, tiled=True))
    cubic = jnp.where(keeping, cubic_sum, jnp.zeros((), jnp.float32))
    return (3.0 * square.astype(jnp.float32) - 2.0 * cubic).astype(jnp.bfloat16)


def solution(mesh):
    placed = (P("row", "col", None, None), P("row", "col"), P("row", "col"))
    return jax.shard_map(
        per_device,
        mesh=mesh,
        in_specs=placed,
        out_specs=P("row", "col", None, None),
        check_vma=False,
    )
```

profile of v0, /device:TPU:1, one launch (start us, length us, event | category | flops | bytes accessed | tf_op | source)
XLA Modules:
  0.0 410.7 jit_solution(9093615501974938881)
XLA Ops:
  6.5 0.7 broadcast_compare_fusion.1
  7.2 0.1 copy.7
  7.3 2.1 broadcast_select_fusion.2
  9.5 1.3 fusion.40
  10.8 3.9 collective-permute-start
  14.8 6.1 %collective-permute-start.1 = (bf16[8,2,128,128]{3,2,1,0:T(8,128)(2,1)S(1)}, bf16[8,2,128,128]{3,2,1,0:T(8,128)(2,1)}, u32[]{:S(2)}, u32[]{:S(2)}) collective-permute-start(bf16[8,2,128,128]{3,2,1,0:T(8,128)(2,1)S(1)} %get-tuple-element.97), channel_id=1, source_target_pairs={{16,0},{32,16},{48,32},{64,48},{80,64},{96,80},{112,96},{128,112},... | collective-permute-start | bytes 1572872 | tf_op jit(solution)/shard_map/ppermute | solution.py:19
  20.9 0.7 broadcast_compare_fusion.2
  21.6 0.1 copy.6
  21.8 0.1 fusion.34
  21.9 0.2 broadcast_convert_fusion
  22.1 3.4 collective-permute-done
  25.5 1.5 collective-permute-done.1
  27.0 1.5 pad_maximum_fusion
  28.5 66.2 %all-gather.3.cloned.1.call-done = bf16[12,32,128,128]{3,2,1,0:T(8,128)(2,1)} async-done(((bf16[12,2,128,128]{3,2,1,0:T(8,128)(2,1)}), bf16[12,32,128,128]{3,2,1,0:T(8,128)(2,1)}) %all-gather.3.cloned.1.call-update) | async-done | bytes 12582928 | tf_op jit(solution)/shard_map/all_gather | solution.py:81
  94.7 113.8 %while.22 = (s32[]{:T(128)}, bf16[4,3,2,128,128]{4,3,2,1,0:T(8,128)(2,1)S(1)}, pred[4,3,2,32]{3,2,1,0:T(4,128)(4,1)S(1)}, s32[4,3,2,32]{3,2,1,0:T(2,128)S(1)}, b...) while((s32[]{:T(128)}, bf16[4,3,2,128,128]{4,3,2,1,0:T(8,128)(2,1)S(1)}, ...), condition=%wide.region_1.3_spmd.clone, body=%wide.region_0.2_spmd.sunk.clone | while | flops 811600576 | bytes 48181520 | solution.py:70
  94.8 7.8 %gather_fusion = bf16[192,128,128]{2,1,0:T(8,128)(2,1)} fusion(bf16[56,128,128]{2,1,0:T(8,128)(2,1)S(1)} %get-tuple-element.222, s32[1024]{0:T(1024)S(1)} %pad_clamp_fusion.6), kind=kCustom, calls=%fused_computation.clone.clone.1.clone | custom fusion | bytes 12583680 | tf_op jit(solution)/shard_map/while/body/eval_jaxpr/jit(_take)/gather | solution.py:63
  102.6 6.0 %broadcast_select_fusion.7 = bf16[192,128,128]{2,1,0:T(8,128)(2,1)} fusion(bf16[192,128,128]{2,1,0:T(8,128)(2,1)} %gather_fusion, pred[192]{0:T(512)(128)(4,1)S(1)} %compare_and_fusion.7), kind=kLoop, calls=%fused_computation.4.clone.1.clone | loop fusion | flops 3145728 | bytes 12583104 | tf_op jit(solution)/shard_map/while/body/eval_jaxpr/jit(_take)/select_n | solution.py:63
  108.6 8.7 %copy.26 = bf16[3,2,32,128,128]{3,4,2,1,0:T(8,128)(2,1)} copy(bf16[3,2,32,128,128]{4,3,2,1,0:T(8,128)(2,1)} %bitcast.78) | data formatting | bytes 12582912 | tf_op jit(solution)/shard_map/while/body/eval_jaxpr/reshape | solution.py:64
  117.3 5.5 %fusion.55 = bf16[1,3,2,128,128]{3,4,2,1,0:T(8,128)(2,1)S(1)} fusion(bf16[4,3,32,128,128]{4,3,2,1,0:T(8,128)(2,1)} %get-tuple-element.223, s32[]{:T(128)} %get-tuple-element.212, bf16[3,2,32,128,128]{3,4,2,1,0:T(8,128)(2,1)} %copy.26, pred[3,2,32]{2,1,0:T(4,128)(4,1)S(1)} %dynamic-slice_bitcast_fusion.6), kind=kOutput, calls=%fused_computation.9.clone.1.clone | convolution fusion | flops 808452096 | bytes 9634496 | tf_op jit(solution)/shard_map/while/body/eval_jaxpr/itab,iftbc->ifac/dot_general | solution.py:66
  122.8 0.2 copy.27
  123.2 7.8 %gather_fusion = bf16[192,128,128]{2,1,0:T(8,128)(2,1)} fusion(bf16[56,128,128]{2,1,0:T(8,128)(2,1)S(1)} %get-tuple-element.222, s32[1024]{0:T(1024)S(1)} %pad_clamp_fusion.6), kind=kCustom, calls=%fused_computation.clone.clone.1.clone | custom fusion | bytes 12583680 | tf_op jit(solution)/shard_map/while/body/eval_jaxpr/jit(_take)/gather | solution.py:63
  131.0 6.0 %broadcast_select_fusion.7 = bf16[192,128,128]{2,1,0:T(8,128)(2,1)} fusion(bf16[192,128,128]{2,1,0:T(8,128)(2,1)} %gather_fusion, pred[192]{0:T(512)(128)(4,1)S(1)} %compare_and_fusion.7), kind=kLoop, calls=%fused_computation.4.clone.1.clone | loop fusion | flops 3145728 | bytes 12583104 | tf_op jit(solution)/shard_map/while/body/eval_jaxpr/jit(_take)/select_n | solution.py:63
  137.0 8.7 %copy.26 = bf16[3,2,32,128,128]{3,4,2,1,0:T(8,128)(2,1)} copy(bf16[3,2,32,128,128]{4,3,2,1,0:T(8,128)(2,1)} %bitcast.78) | data formatting | bytes 12582912 | tf_op jit(solution)/shard_map/while/body/eval_jaxpr/reshape | solution.py:64
  145.7 5.5 %fusion.55 = bf16[1,3,2,128,128]{3,4,2,1,0:T(8,128)(2,1)S(1)} fusion(bf16[4,3,32,128,128]{4,3,2,1,0:T(8,128)(2,1)} %get-tuple-element.223, s32[]{:T(128)} %get-tuple-element.212, bf16[3,2,32,128,128]{3,4,2,1,0:T(8,128)(2,1)} %copy.26, pred[3,2,32]{2,1,0:T(4,128)(4,1)S(1)} %dynamic-slice_bitcast_fusion.6), kind=kOutput, calls=%fused_computation.9.clone.1.clone | convolution fusion | flops 808452096 | bytes 9634496 | tf_op jit(solution)/shard_map/while/body/eval_jaxpr/itab,iftbc->ifac/dot_general | solution.py:66
  151.3 0.2 copy.27
  151.6 7.8 %gather_fusion = bf16[192,128,128]{2,1,0:T(8,128)(2,1)} fusion(bf16[56,128,128]{2,1,0:T(8,128)(2,1)S(1)} %get-tuple-element.222, s32[1024]{0:T(1024)S(1)} %pad_clamp_fusion.6), kind=kCustom, calls=%fused_computation.clone.clone.1.clone | custom fusion | bytes 12583680 | tf_op jit(solution)/shard_map/while/body/eval_jaxpr/jit(_take)/gather | solution.py:63
  159.4 6.0 %broadcast_select_fusion.7 = bf16[192,128,128]{2,1,0:T(8,128)(2,1)} fusion(bf16[192,128,128]{2,1,0:T(8,128)(2,1)} %gather_fusion, pred[192]{0:T(512)(128)(4,1)S(1)} %compare_and_fusion.7), kind=kLoop, calls=%fused_computation.4.clone.1.clone | loop fusion | flops 3145728 | bytes 12583104 | tf_op jit(solution)/shard_map/while/body/eval_jaxpr/jit(_take)/select_n | solution.py:63
  165.5 8.7 %copy.26 = bf16[3,2,32,128,128]{3,4,2,1,0:T(8,128)(2,1)} copy(bf16[3,2,32,128,128]{4,3,2,1,0:T(8,128)(2,1)} %bitcast.78) | data formatting | bytes 12582912 | tf_op jit(solution)/shard_map/while/body/eval_jaxpr/reshape | solution.py:64
  174.2 5.5 %fusion.55 = bf16[1,3,2,128,128]{3,4,2,1,0:T(8,128)(2,1)S(1)} fusion(bf16[4,3,32,128,128]{4,3,2,1,0:T(8,128)(2,1)} %get-tuple-element.223, s32[]{:T(128)} %get-tuple-element.212, bf16[3,2,32,128,128]{3,4,2,1,0:T(8,128)(2,1)} %copy.26, pred[3,2,32]{2,1,0:T(4,128)(4,1)S(1)} %dynamic-slice_bitcast_fusion.6), kind=kOutput, calls=%fused_computation.9.clone.1.clone | convolution fusion | flops 808452096 | bytes 9634496 | tf_op jit(solution)/shard_map/while/body/eval_jaxpr/itab,iftbc->ifac/dot_general | solution.py:66
  179.7 0.2 copy.27
  180.0 7.9 %gather_fusion = bf16[192,128,128]{2,1,0:T(8,128)(2,1)} fusion(bf16[56,128,128]{2,1,0:T(8,128)(2,1)S(1)} %get-tuple-element.222, s32[1024]{0:T(1024)S(1)} %pad_clamp_fusion.6), kind=kCustom, calls=%fused_computation.clone.clone.1.clone | custom fusion | bytes 12583680 | tf_op jit(solution)/shard_map/while/body/eval_jaxpr/jit(_take)/gather | solution.py:63
  187.9 6.0 %broadcast_select_fusion.7 = bf16[192,128,128]{2,1,0:T(8,128)(2,1)} fusion(bf16[192,128,128]{2,1,0:T(8,128)(2,1)} %gather_fusion, pred[192]{0:T(512)(128)(4,1)S(1)} %compare_and_fusion.7), kind=kLoop, calls=%fused_computation.4.clone.1.clone | loop fusion | flops 3145728 | bytes 12583104 | tf_op jit(solution)/shard_map/while/body/eval_jaxpr/jit(_take)/select_n | solution.py:63
  194.0 8.7 %copy.26 = bf16[3,2,32,128,128]{3,4,2,1,0:T(8,128)(2,1)} copy(bf16[3,2,32,128,128]{4,3,2,1,0:T(8,128)(2,1)} %bitcast.78) | data formatting | bytes 12582912 | tf_op jit(solution)/shard_map/while/body/eval_jaxpr/reshape | solution.py:64
  202.7 5.5 %fusion.55 = bf16[1,3,2,128,128]{3,4,2,1,0:T(8,128)(2,1)S(1)} fusion(bf16[4,3,32,128,128]{4,3,2,1,0:T(8,128)(2,1)} %get-tuple-element.223, s32[]{:T(128)} %get-tuple-element.212, bf16[3,2,32,128,128]{3,4,2,1,0:T(8,128)(2,1)} %copy.26, pred[3,2,32]{2,1,0:T(4,128)(4,1)S(1)} %dynamic-slice_bitcast_fusion.6), kind=kOutput, calls=%fused_computation.9.clone.1.clone | convolution fusion | flops 808452096 | bytes 9634496 | tf_op jit(solution)/shard_map/while/body/eval_jaxpr/itab,iftbc->ifac/dot_general | solution.py:66
  208.2 0.2 copy.27
  208.4 1.1 fusion.29
  209.6 77.2 %all-gather.5.cloned.1.call-done = bf16[12,32,128,128]{3,2,1,0:T(8,128)(2,1)} async-done(((bf16[12,2,128,128]{3,2,1,0:T(8,128)(2,1)}), bf16[12,32,128,128]{3,2,1,0:T(8,128)(2,1)}) %all-gather.5.cloned.1.call-update) | async-done | bytes 12582928 | tf_op jit(solution)/shard_map/all_gather | solution.py:83
  286.7 114.3 %while.23 = (s32[]{:T(128)}, f32[4,3,2,128,128]{4,3,2,1,0:T(8,128)}, pred[4,3,2,32]{3,2,1,0:T(4,128)(4,1)S(1)}, s32[4,3,2,32]{3,2,1,0:T(2,128)S(1)}, bf16[56,128...) while((s32[]{:T(128)}, f32[4,3,2,128,128]{4,3,2,1,0:T(8,128)}, ...), condition=%wide.region_3.5_spmd.clone, body=%wide.region_2.4_spmd.sunk.clone | while | flops 811600576 | bytes 49165068 | solution.py:70
  286.7 0.1 reshape.347
  286.8 7.8 %gather_fusion.1 = bf16[192,128,128]{2,1,0:T(8,128)(2,1)} fusion(bf16[56,128,128]{2,1,0:T(8,128)(2,1)S(1)} %get-tuple-element.240, s32[1024]{0:T(1024)S(1)} %pad_clamp_fusion.7), kind=kCustom, calls=%fused_computation.1.clone.clone.1.clone | custom fusion | bytes 12583680 | tf_op jit(solution)/shard_map/while/body/eval_jaxpr/jit(_take)/gather | solution.py:63
  294.7 6.0 %broadcast_select_fusion.8 = bf16[192,128,128]{2,1,0:T(8,128)(2,1)} fusion(bf16[192,128,128]{2,1,0:T(8,128)(2,1)} %gather_fusion.1, pred[192]{0:T(512)(128)(4,1)S(1)} %compare_and_fusion.8), kind=kLoop, calls=%fused_computation.20.clone.1.clone | loop fusion | flops 3145728 | bytes 12583104 | tf_op jit(solution)/shard_map/while/body/eval_jaxpr/jit(_take)/select_n | solution.py:63
  300.7 8.7 %copy.28 = bf16[3,2,32,128,128]{3,4,2,1,0:T(8,128)(2,1)} copy(bf16[3,2,32,128,128]{4,3,2,1,0:T(8,128)(2,1)} %bitcast.79) | data formatting | bytes 12582912 | tf_op jit(solution)/shard_map/while/body/eval_jaxpr/reshape | solution.py:64
  309.4 4.9 %fusion.58 = f32[1,3,2,128,128]{3,4,2,1,0:T(8,128)S(1)} fusion(bf16[4,3,32,128,128]{4,3,2,1,0:T(8,128)(2,1)} %get-tuple-element.241, s32[]{:T(128)} %get-tuple-element.230, bf16[3,2,32,128,128]{3,4,2,1,0:T(8,128)(2,1)} %copy.28, pred[3,2,32]{2,1,0:T(4,128)(4,1)S(1)} %dynamic-slice_bitcast_fusion.7), kind=kOutput, calls=%fused_computation.25.clone.1.clone | convolution fusion | flops 808452096 | bytes 9831104 | tf_op jit(solution)/shard_map/while/body/eval_jaxpr/itab,iftbc->ifac/dot_general | solution.py:66
  314.3 0.2 copy.29
  314.5 0.8 constant_dynamic-update-slice_fusion.7
  315.4 7.8 %gather_fusion.1 = bf16[192,128,128]{2,1,0:T(8,128)(2,1)} fusion(bf16[56,128,128]{2,1,0:T(8,128)(2,1)S(1)} %get-tuple-element.240, s32[1024]{0:T(1024)S(1)} %pad_clamp_fusion.7), kind=kCustom, calls=%fused_computation.1.clone.clone.1.clone | custom fusion | bytes 12583680 | tf_op jit(solution)/shard_map/while/body/eval_jaxpr/jit(_take)/gather | solution.py:63
  323.2 6.0 %broadcast_select_fusion.8 = bf16[192,128,128]{2,1,0:T(8,128)(2,1)} fusion(bf16[192,128,128]{2,1,0:T(8,128)(2,1)} %gather_fusion.1, pred[192]{0:T(512)(128)(4,1)S(1)} %compare_and_fusion.8), kind=kLoop, calls=%fused_computation.20.clone.1.clone | loop fusion | flops 3145728 | bytes 12583104 | tf_op jit(solution)/shard_map/while/body/eval_jaxpr/jit(_take)/select_n | solution.py:63
  329.2 8.7 %copy.28 = bf16[3,2,32,128,128]{3,4,2,1,0:T(8,128)(2,1)} copy(bf16[3,2,32,128,128]{4,3,2,1,0:T(8,128)(2,1)} %bitcast.79) | data formatting | bytes 12582912 | tf_op jit(solution)/shard_map/while/body/eval_jaxpr/reshape | solution.py:64
  337.9 4.9 %fusion.58 = f32[1,3,2,128,128]{3,4,2,1,0:T(8,128)S(1)} fusion(bf16[4,3,32,128,128]{4,3,2,1,0:T(8,128)(2,1)} %get-tuple-element.241, s32[]{:T(128)} %get-tuple-element.230, bf16[3,2,32,128,128]{3,4,2,1,0:T(8,128)(2,1)} %copy.28, pred[3,2,32]{2,1,0:T(4,128)(4,1)S(1)} %dynamic-slice_bitcast_fusion.7), kind=kOutput, calls=%fused_computation.25.clone.1.clone | convolution fusion | flops 808452096 | bytes 9831104 | tf_op jit(solution)/shard_map/while/body/eval_jaxpr/itab,iftbc->ifac/dot_general | solution.py:66
  342.9 0.2 copy.29
  343.1 0.8 constant_dynamic-update-slice_fusion.7
  344.0 7.8 %gather_fusion.1 = bf16[192,128,128]{2,1,0:T(8,128)(2,1)} fusion(bf16[56,128,128]{2,1,0:T(8,128)(2,1)S(1)} %get-tuple-element.240, s32[1024]{0:T(1024)S(1)} %pad_clamp_fusion.7), kind=kCustom, calls=%fused_computation.1.clone.clone.1.clone | custom fusion | bytes 12583680 | tf_op jit(solution)/shard_map/while/body/eval_jaxpr/jit(_take)/gather | solution.py:63
  351.8 6.0 %broadcast_select_fusion.8 = bf16[192,128,128]{2,1,0:T(8,128)(2,1)} fusion(bf16[192,128,128]{2,1,0:T(8,128)(2,1)} %gather_fusion.1, pred[192]{0:T(512)(128)(4,1)S(1)} %compare_and_fusion.8), kind=kLoop, calls=%fused_computation.20.clone.1.clone | loop fusion | flops 3145728 | bytes 12583104 | tf_op jit(solution)/shard_map/while/body/eval_jaxpr/jit(_take)/select_n | solution.py:63
  357.8 8.7 %copy.28 = bf16[3,2,32,128,128]{3,4,2,1,0:T(8,128)(2,1)} copy(bf16[3,2,32,128,128]{4,3,2,1,0:T(8,128)(2,1)} %bitcast.79) | data formatting | bytes 12582912 | tf_op jit(solution)/shard_map/while/body/eval_jaxpr/reshape | solution.py:64
  366.5 5.0 %fusion.58 = f32[1,3,2,128,128]{3,4,2,1,0:T(8,128)S(1)} fusion(bf16[4,3,32,128,128]{4,3,2,1,0:T(8,128)(2,1)} %get-tuple-element.241, s32[]{:T(128)} %get-tuple-element.230, bf16[3,2,32,128,128]{3,4,2,1,0:T(8,128)(2,1)} %copy.28, pred[3,2,32]{2,1,0:T(4,128)(4,1)S(1)} %dynamic-slice_bitcast_fusion.7), kind=kOutput, calls=%fused_computation.25.clone.1.clone | convolution fusion | flops 808452096 | bytes 9831104 | tf_op jit(solution)/shard_map/while/body/eval_jaxpr/itab,iftbc->ifac/dot_general | solution.py:66
  371.5 0.2 copy.29
  371.7 0.8 constant_dynamic-update-slice_fusion.7
  372.5 7.9 %gather_fusion.1 = bf16[192,128,128]{2,1,0:T(8,128)(2,1)} fusion(bf16[56,128,128]{2,1,0:T(8,128)(2,1)S(1)} %get-tuple-element.240, s32[1024]{0:T(1024)S(1)} %pad_clamp_fusion.7), kind=kCustom, calls=%fused_computation.1.clone.clone.1.clone | custom fusion | bytes 12583680 | tf_op jit(solution)/shard_map/while/body/eval_jaxpr/jit(_take)/gather | solution.py:63
  380.4 6.0 %broadcast_select_fusion.8 = bf16[192,128,128]{2,1,0:T(8,128)(2,1)} fusion(bf16[192,128,128]{2,1,0:T(8,128)(2,1)} %gather_fusion.1, pred[192]{0:T(512)(128)(4,1)S(1)} %compare_and_fusion.8), kind=kLoop, calls=%fused_computation.20.clone.1.clone | loop fusion | flops 3145728 | bytes 12583104 | tf_op jit(solution)/shard_map/while/body/eval_jaxpr/jit(_take)/select_n | solution.py:63
  386.5 8.7 %copy.28 = bf16[3,2,32,128,128]{3,4,2,1,0:T(8,128)(2,1)} copy(bf16[3,2,32,128,128]{4,3,2,1,0:T(8,128)(2,1)} %bitcast.79) | data formatting | bytes 12582912 | tf_op jit(solution)/shard_map/while/body/eval_jaxpr/reshape | solution.py:64
  395.2 5.0 %fusion.58 = f32[1,3,2,128,128]{3,4,2,1,0:T(8,128)S(1)} fusion(bf16[4,3,32,128,128]{4,3,2,1,0:T(8,128)(2,1)} %get-tuple-element.241, s32[]{:T(128)} %get-tuple-element.230, bf16[3,2,32,128,128]{3,4,2,1,0:T(8,128)(2,1)} %copy.28, pred[3,2,32]{2,1,0:T(4,128)(4,1)S(1)} %dynamic-slice_bitcast_fusion.7), kind=kOutput, calls=%fused_computation.25.clone.1.clone | convolution fusion | flops 808452096 | bytes 9831104 | tf_op jit(solution)/shard_map/while/body/eval_jaxpr/itab,iftbc->ifac/dot_general | solution.py:66
  400.1 0.2 copy.29
  400.3 0.8 constant_dynamic-update-slice_fusion.7
  401.1 2.7 fusion.28
  (62 shorter events, 1.2 us)
Async XLA Ops:
  6.5 88.1 %all-gather.3.cloned.1.call-start = ((), (), s32[]{:S(2)}) async-start(), calls=%async_computation | async-start | bytes 13369344 | tf_op jit(solution)/shard_map/all_gather | solution.py:81
  9.5 277.2 %all-gather.5.cloned.1.call-start = ((), (), s32[]{:S(2)}) async-start(), calls=%async_computation.1 | async-start | bytes 13369344 | tf_op jit(solution)/shard_map/all_gather | solution.py:83
  10.8 14.7 %collective-permute-start = (bf16[8,2,128,128]{3,2,1,0:T(8,128)(2,1)S(1)}, bf16[8,2,128,128]{3,2,1,0:T(8,128)(2,1)S(1)}, u32[]{:S(2)}, u32[]{:S(2)}) collective-permute-start(bf16[8,2,128,128]{3,2,1,0:T(8,128)(2,1)S(1)} %get-tuple-element.96), channel_id=1, source_target_pairs={{0,16},{16,32},{32,48},{48,64},{64,80},{80,96},{96,112},{112,128},... | collective-permute-start | bytes 1572872 | tf_op jit(solution)/shard_map/ppermute | solution.py:18
  14.8 12.2 %collective-permute-start.1 = (bf16[8,2,128,128]{3,2,1,0:T(8,128)(2,1)S(1)}, bf16[8,2,128,128]{3,2,1,0:T(8,128)(2,1)}, u32[]{:S(2)}, u32[]{:S(2)}) collective-permute-start(bf16[8,2,128,128]{3,2,1,0:T(8,128)(2,1)S(1)} %get-tuple-element.97), channel_id=1, source_target_pairs={{16,0},{32,16},{48,32},{64,48},{80,64},{96,80},{112,96},{128,112},... | collective-permute-start | bytes 1572872 | tf_op jit(solution)/shard_map/ppermute | solution.py:19
Sparse Core Ops, SparseCore 0:
  9.6 84.9 all-gather.2
  209.7 77.0 all-gather.4
where the time goes:
time: 413 us; the launch traced here: 411 us
  waiting for transfers between devices  148 us (36%)
  local copies, waits for them, and re-layouts  139 us (34%)
  other arithmetic  57.6 us (14%)
  matrix products  42 us (10%)
  between operations  13.5 us (3%)
  starting transfers between devices  10.1 us (2%)
    all_gather x1, waiting for transfers between devices, per_device(): cubic_sum = accumulate(lax.all_gather(square, 'col', axis=1, tiled=True))  77.2 us
    reshape x8, local copies, waits for them, and re-layouts, one_block(): fetched = fetched.reshape(index_block.shape + (tile_size, tile_size))  69.5 us
    all_gather x1, waiting for transfers between devices, per_device(): square_sum = accumulate(lax.all_gather(masked, 'col', axis=1, tiled=True))  66.2 us
    gather x8, local copies, waits for them, and re-layouts, one_block(): fetched = jnp.take(table_flat, index_block.reshape(-1), axis=0)  62.6 us
    select_n x16, other arithmetic, one_block(): fetched = jnp.take(table_flat, index_block.reshape(-1), axis=0)  48.2 us
    dot_general x8, matrix products, one_block(): jnp.einsum('itab,iftbc->ifac', piece_block, fetched, preferred_element_ty...  42 us
  transfers between devices with their start and end apart: 4, of which 4 were waited for; matrix products, arithmetic and copies ran while one was open for 1% of the time, Pallas kernels for 0%

commit v1 on v0

v1 whole, which is shorter than its diff:
```python
import functools

import jax
import jax.numpy as jnp
import numpy as np
from jax import lax
from jax.experimental import pallas as pl
from jax.experimental.pallas import tpu as pltpu
from jax.sharding import PartitionSpec as P

W = 8
EARLY = 8
LATE = 6


def assign(rows, groups):
    size = rows + 2 * W
    items = [(u, v) for u in range(size) for v in range(u, min(size, u + W + 1))]

    def seats(pair):
        found = []
        for w, j in dict.fromkeys((pair, pair[::-1])):
            kind = 0 if W <= w < W + rows else 1
            found.append(((j % groups, kind), (w, j)))
        return sorted(found)

    room = {0: EARLY, 1: LATE}
    taken = {(m, kind): [] for m in range(groups) for kind in (0, 1)}

    def place(pair, seen):
        for seat, tile in seats(pair):
            if seat in seen:
                continue
            seen.add(seat)
            if len(taken[seat]) < room[seat[1]]:
                taken[seat].append((pair, tile))
                return True
            for index, (other, _) in enumerate(taken[seat]):
                if place(other, seen):
                    taken[seat][index] = (pair, tile)
                    return True
        return False

    for pair in items:
        if not place(pair, set()):
            raise ValueError("no room")
    early = [sorted(tile for _, tile in taken[m, 0]) for m in range(groups)]
    late = [sorted(tile for _, tile in taken[m, 1]) for m in range(groups)]
    return early, late


def slot_of(w, j, first):
    return (w - first) * 2 + (1 if j - w == W else 0)


def tables(early, late, rows, groups):
    out = np.full((groups, EARLY + 2 * LATE), -1, np.int32)
    for m in range(groups):
        for e, (w, j) in enumerate(early[m]):
            out[m, e] = slot_of(w, j, W)
        for e, (w, j) in enumerate(late[m]):
            if w < W:
                out[m, EARLY + e] = slot_of(w, j, W - rows)
            else:
                out[m, EARLY + LATE + e] = slot_of(w, j, W + rows)
    return out.reshape(-1)


def relative(row_index, col_index, rows, groups):
    return lax.rem(col_index - row_index * rows + W + groups * rows * 64, groups)


def pack_kernel(rows, groups, table, pattern, keep, density, early, up, down):
    size = density.shape[-1]
    width = EARLY + 2 * LATE
    r = lax.axis_index("row")
    c = lax.axis_index("col")
    own = relative(r, c, rows, groups)
    after = relative(r + 1, c, rows, groups)
    before = relative(r + lax.axis_size("row") - 1, c, rows, groups)

    def move(target, e, slot):
        safe = jnp.maximum(slot, 0)
        used = (slot >= 0) & (pattern[safe // 2, lax.rem(safe, 2)] == 1)
        tile = density[safe]
        target[pl.ds(e * size, size), :] = jnp.where(used, tile, jnp.zeros_like(tile))

    for e in range(EARLY):
        move(early, e, table[own * width + e])
    for e in range(LATE):
        move(up, e, table[after * width + EARLY + e])
        move(down, e, table[before * width + EARLY + LATE + e])
    flags = jnp.zeros((32, size), jnp.float32)
    line = lax.broadcasted_iota(jnp.int32, (32, size), 0)
    for a in range(rows):
        for q in range(2):
            value = jnp.where(keep[a, q] == 1, 1.0, 0.0)
            flags = jnp.where(line == a * 2 + q, value, flags)
    early[pl.ds(EARLY * size, 32), :] = flags.astype(jnp.bfloat16)


def multiply_kernel(rows, groups, early_tiles, late_tiles, keep, gathered, out, dense, square, columns, flags):
    size = out.shape[-1]
    window = rows + 2 * W
    r = lax.axis_index("row")
    c = lax.axis_index("col")
    m = relative(r, c, rows, groups)
    turn = lax.rem(c - m + groups, groups)
    pair = 2 * size
    half = W // 2
    supers = window // 2

    nothing = jnp.zeros((size, size), jnp.bfloat16)
    for u in range(window):
        for v in range(window):
            if abs(u - v) > W and abs(u // 2 - v // 2) <= half:
                dense[pl.ds(u * size, size), pl.ds(v * size, size)] = nothing
    for n in range(groups):
        p = lax.rem(turn + n, groups)
        for e, (w, j) in enumerate(early_tiles[n] + late_tiles[n]):
            line = e * size if e < len(early_tiles[n]) else (EARLY + e - len(early_tiles[n])) * size + 32
            tile = gathered[p, pl.ds(line, size), :]
            dense[pl.ds(w * size, size), pl.ds(j * size, size)] = tile
            if w != j:
                dense[pl.ds(j * size, size), pl.ds(w * size, size)] = tile.T
        flags[pl.ds(n * 32, 32), :] = gathered[p, pl.ds(EARLY * size, 32), :].astype(jnp.float32)

    first = pl.multiple_of(m * size, size)
    second = pl.multiple_of(jnp.minimum(m + groups, window - 1) * size, size)
    columns[...] = jnp.zeros_like(columns)
    for j, start, place in ((m, first, 0), (jnp.minimum(m + groups, window - 1), second, size)):
        for u in range(window):
            inside = (u - j <= W) & (j - u <= W)

            @pl.when(inside)
            def _():
                columns[pl.ds(u * size, size), pl.ds(place, size)] = dense[pl.ds(u * size, size), pl.ds(start, size)]

    for step in range(rows // 2):
        top = half + step
        line = top * pair
        for other in range(top - half, top + half + 1):
            low = max(top, other) - half
            high = min(top, other) + half + 1
            product = jnp.dot(
                dense[pl.ds(line, pair), pl.ds(low * pair, (high - low) * pair)],
                dense[pl.ds(low * pair, (high - low) * pair), pl.ds(other * pair, pair)],
                preferred_element_type=jnp.float32,
            )
            for x in range(2):
                for y in range(2):
                    a, k = 2 * step + x, 2 * other + y
                    d = k - (a + W)
                    if abs(d) > W:
                        tile = jnp.zeros((size, size), jnp.bfloat16)
                    else:
                        flag = flags[pl.ds((k % groups) * 32 + a * 2 + (1 if d == W else 0), 1), :]
                        tile = product[x * size : (x + 1) * size, y * size : (y + 1) * size]
                        tile = jnp.where(flag > 0.5, tile, 0.0).astype(jnp.bfloat16)
                    square[pl.ds(a * size, size), pl.ds(k * size, size)] = tile
        low = (top - half) * pair
        deep = (2 * half + 1) * pair
        cubic = jnp.dot(
            square[pl.ds(step * pair, pair), pl.ds(low, deep)],
            columns[pl.ds(low, deep), :],
            preferred_element_type=jnp.float32,
        )
        for x in range(2):
            a = 2 * step + x
            upper = a <= m
            start = jnp.where(upper, first, second)
            start = pl.multiple_of(start, size)
            third = cubic[x * size : (x + 1) * size, :]
            chosen = jnp.where(upper, third[:, :size], third[:, size:])
            base = square[pl.ds(a * size, size), pl.ds(start, size)].astype(jnp.float32)
            value = 3.0 * base - 2.0 * chosen
            out[2 * a] = jnp.where(keep[a, 0] == 1, value, 0.0).astype(out.dtype)
            there = (keep[a, 1] == 1) & (a == m)
            base = square[pl.ds(a * size, size), pl.ds(second, size)].astype(jnp.float32)
            value = 3.0 * base - 2.0 * third[:, size:]
            out[2 * a + 1] = jnp.where(there, value, 0.0).astype(out.dtype)


def per_device(density, density_pattern, filter_pattern):
    rows, slots, size, _ = density.shape
    groups = lax.axis_size("col")
    count = lax.axis_size("row")
    early_tiles, late_tiles = assign(rows, groups)
    table = jnp.asarray(tables(early_tiles, late_tiles, rows, groups))
    window = rows + 2 * W
    smem = pl.BlockSpec(memory_space=pltpu.SMEM)
    vmem = pl.BlockSpec(memory_space=pltpu.VMEM)
    early, up, down = pl.pallas_call(
        functools.partial(pack_kernel, rows, groups),
        out_shape=[
            jax.ShapeDtypeStruct((EARLY * size + 32, size), jnp.bfloat16),
            jax.ShapeDtypeStruct((LATE * size, size), jnp.bfloat16),
            jax.ShapeDtypeStruct((LATE * size, size), jnp.bfloat16),
        ],
        in_specs=[smem, smem, smem, vmem],
        out_specs=[vmem, vmem, vmem],
        name="pack",
    )(table, density_pattern, filter_pattern, density.reshape(rows * slots, size, size))
    forward = [(i, (i + 1) % count) for i in range(count)]
    backward = [(j, i) for i, j in forward]
    late = lax.ppermute(up, "row", forward) + lax.ppermute(down, "row", backward)
    mine = jnp.concatenate([early, late], axis=0)
    gathered = lax.all_gather(mine, "col", axis=0, tiled=False)
    out = pl.pallas_call(
        functools.partial(multiply_kernel, rows, groups, early_tiles, late_tiles),
        out_shape=jax.ShapeDtypeStruct((rows * slots, size, size), jnp.bfloat16),
        in_specs=[smem, vmem],
        out_specs=vmem,
        scratch_shapes=[
            pltpu.VMEM((window * size, window * size), jnp.bfloat16),
            pltpu.VMEM((rows * size, window * size), jnp.bfloat16),
            pltpu.VMEM((window * size, 2 * size), jnp.bfloat16),
            pltpu.VMEM((groups * 32, size), jnp.float32),
        ],
        compiler_params=pltpu.CompilerParams(vmem_limit_bytes=60 * 1024 * 1024),
        name="multiply",
    )(filter_pattern, gathered)
    return out.reshape(rows, slots, size, size)


def solution(mesh):
    placed = (P("row", "col", None, None), P("row", "col"), P("row", "col"))
    return jax.shard_map(
        per_device,
        mesh=mesh,
        in_specs=placed,
        out_specs=P("row", "col", None, None),
        check_vma=False,
    )
```

time: 413 us -> 117 us (0.28)
  local copies, waits for them, and re-layouts: 139 us -> 2.7 us
  waiting for transfers between devices: 148 us -> 65 us
  other arithmetic: 57.6 us -> 1.81 us
  matrix products: 42 us -> 0 us
  Pallas kernels: 0 us -> 24.2 us
    all_gather x2 -> x1, waiting for transfers between devices: 143 us -> 62 us  [per_device(): gathered = lax.all_gather(mine, 'col', axis=0, tiled=False)]
    reshape x16 -> x0, local copies, waits for them, and re-layouts: 70.2 us -> none  [the longest x8 69.5 us: one_block(): fetched = fetched.reshape(index_block.shape + (tile_size, tile_size))]
    gather x8 -> x0, local copies, waits for them, and re-layouts: 62.6 us -> none  [one_block(): fetched = jnp.take(table_flat, index_block.reshape(-1), axis=0)]
    select_n x19 -> x0, other arithmetic: 50.4 us -> none  [the longest x16 48.2 us: one_block(): fetched = jnp.take(table_flat, index_block.reshape(-1), axis=0)]
    dot_general x8 -> x0, matrix products: 42 us -> none  [one_block(): jnp.einsum('itab,iftbc->ifac', piece_block, fetched, preferred_element_ty...]
    pallas_call x0 -> x2, Pallas kernels: none -> 24.2 us  [the longest x1 22 us: per_device(): pl.pallas_call(functools.partial(multiply_kernel, rows, groups, early_til...]
    dynamic_update_slice x16 -> x0, local copies, waits for them, and re-layouts: 4.66 us -> none  [accumulate(): lax.map(one_block, (panel_piece.reshape(block_count, block_rows, piece_wi...]
  transfers between devices with their start and end apart: 4 -> 3, of which waited for: 4 -> 3; matrix products, arithmetic and copies ran while one was open for 1% -> 0% of each run, Pallas kernels for 0% -> 0%
where the time goes in v1:
time: 117 us
  waiting for transfers between devices  65 us (56%)
  Pallas kernels  24.2 us (21%)
  between operations  13.4 us (11%)
  starting transfers between devices  10 us (9%)
  local copies, waits for them, and re-layouts  2.7 us (2%)
  other arithmetic  1.81 us (2%)
    all_gather x1, waiting for transfers between devices, per_device(): gathered = lax.all_gather(mine, 'col', axis=0, tiled=False)  62 us
    pallas_call x1, Pallas kernels, per_device(): pl.pallas_call(functools.partial(multiply_kernel, rows, groups, early_til...  22 us
    ppermute x1, starting transfers between devices, per_device(): lax.ppermute(down, 'row', backward)  6.09 us
    ppermute x1, starting transfers between devices, per_device(): lax.ppermute(up, 'row', forward) + lax.ppermute(down, 'row', backward)  3.94 us
    unnamed x2, local copies, waits for them, and re-layouts  2.7 us
  transfers between devices with their start and end apart: 3, of which 3 were waited for; matrix products, arithmetic and copies ran while one was open for 0% of the time, Pallas kernels for 0%

profile of v1, /device:TPU:1, one launch (start us, length us, event | category | flops | bytes accessed | tf_op | source)
XLA Modules:
  0.0 117.1 jit_solution(520726223822145050)
XLA Ops:
  6.5 0.0 all-gather.3.cloned.1.call-start
  6.5 1.3 %copy.7.keep = s32[12,2]{1,0:T(8,128)} copy(s32[12,2]{0,1:T(2,128)} %param.6) | data formatting | bytes 192 | tf_op args[2]
  7.9 1.4 %copy.5.pattern = s32[12,2]{1,0:T(8,128)} copy(s32[12,2]{0,1:T(2,128)} %param.5) | data formatting | bytes 192 | tf_op args[1]
  9.2 2.2 %pack.1 = (bf16[1056,128]{1,0:T(8,128)(2,1)}, bf16[768,128]{1,0:T(8,128)(2,1)}, bf16[768,128]{1,0:T(8,128)(2,1)}) custom-call(s32[320]{0:T(512)} %constant.2.clone.table, s32[12,2]{1,0:T(8,128)} %copy.5.pattern, s32[12,2]{1,0:T(8,128)} %copy.7.keep, bf16[24,128,128]{2,1,0:T(8,128)(2,1)} %bitcast.4), custom_call_target="tpu_custom_call" | custom-call | tf_op jit(solution)/shard_map/pack/pallas_call | solution.py:193
  11.5 3.9 %collective-permute-start = (bf16[768,128]{1,0:T(8,128)(2,1)}, bf16[768,128]{1,0:T(8,128)(2,1)S(1)}, u32[]{:S(2)}, u32[]{:S(2)}) collective-permute-start(bf16[768,128]{1,0:T(8,128)(2,1)} %get-tuple-element.9), channel_id=1, source_target_pairs={{0,16},{16,32},{32,48},{48,64},{64,80},{80,96},{96,112},{112,128},... | collective-permute-start | bytes 589832 | tf_op jit(solution)/shard_map/ppermute | solution.py:206
  15.4 6.1 %collective-permute-start.1 = (bf16[768,128]{1,0:T(8,128)(2,1)}, bf16[768,128]{1,0:T(8,128)(2,1)S(1)}, u32[]{:S(2)}, u32[]{:S(2)}) collective-permute-start(bf16[768,128]{1,0:T(8,128)(2,1)} %get-tuple-element.10), channel_id=1, source_target_pairs={{16,0},{32,16},{48,32},{64,48},{80,64},{96,80},{112,96},{128,112},... | collective-permute-start | bytes 589832 | tf_op jit(solution)/shard_map/ppermute | solution.py:206
  21.5 1.3 %collective-permute-done = bf16[768,128]{1,0:T(8,128)(2,1)S(1)} collective-permute-done((bf16[768,128]{1,0:T(8,128)(2,1)}, bf16[768,128]{1,0:T(8,128)(2,1)S(1)}, u32[]{:S(2)}, u32[]{:S(2)}) %collective-permute-start) | collective-permute-done | bytes 196640 | tf_op jit(solution)/shard_map/ppermute | solution.py:206
  22.8 1.6 %collective-permute-done.1 = bf16[768,128]{1,0:T(8,128)(2,1)S(1)} collective-permute-done((bf16[768,128]{1,0:T(8,128)(2,1)}, bf16[768,128]{1,0:T(8,128)(2,1)S(1)}, u32[]{:S(2)}, u32[]{:S(2)}) %collective-permute-start.1) | collective-permute-done | bytes 196640 | tf_op jit(solution)/shard_map/ppermute | solution.py:206
  24.4 0.1 add.3
  24.5 1.8 %pad_maximum_fusion = bf16[1824,128]{1,0:T(8,128)(2,1)} fusion(bf16[768,128]{1,0:T(8,128)(2,1)S(1)} %add.3, bf16[1056,128]{1,0:T(8,128)(2,1)} %get-tuple-element.8), kind=kLoop, calls=%fused_computation | loop fusion | flops 933888 | bytes 933888 | tf_op jit(solution)/shard_map/concatenate | solution.py:207
  26.2 0.0 all-gather.3.cloned.1.call-update
  26.3 62.0 %all-gather.3.cloned.1.call-done = bf16[29184,128]{1,0:T(8,128)(2,1)} async-done(((bf16[1824,128]{1,0:T(8,128)(2,1)}), bf16[29184,128]{1,0:T(8,128)(2,1)}) %all-gather.3.cloned.1.call-update) | async-done | bytes 7471120 | tf_op jit(solution)/shard_map/all_gather | solution.py:208
  88.3 22.0 %multiply.1 = bf16[24,128,128]{2,1,0:T(8,128)(2,1)} custom-call(s32[12,2]{1,0:T(8,128)} %copy.7.keep, bf16[16,1824,128]{2,1,0:T(8,128)(2,1)} %bitcast.3), custom_call_target="tpu_custom_call" | custom-call | tf_op jit(solution)/shard_map/multiply/pallas_call | solution.py:209
Async XLA Ops:
  6.5 81.8 %all-gather.3.cloned.1.call-start = ((), (), s32[]{:S(2)}) async-start(), calls=%async_computation | async-start | bytes 7938048 | tf_op jit(solution)/shard_map/all_gather | solution.py:208
  11.5 11.4 %collective-permute-start = (bf16[768,128]{1,0:T(8,128)(2,1)}, bf16[768,128]{1,0:T(8,128)(2,1)S(1)}, u32[]{:S(2)}, u32[]{:S(2)}) collective-permute-start(bf16[768,128]{1,0:T(8,128)(2,1)} %get-tuple-element.9), channel_id=1, source_target_pairs={{0,16},{16,32},{32,48},{48,64},{64,80},{80,96},{96,112},{112,128},... | collective-permute-start | bytes 589832 | tf_op jit(solution)/shard_map/ppermute | solution.py:206
  15.4 9.0 %collective-permute-start.1 = (bf16[768,128]{1,0:T(8,128)(2,1)}, bf16[768,128]{1,0:T(8,128)(2,1)S(1)}, u32[]{:S(2)}, u32[]{:S(2)}) collective-permute-start(bf16[768,128]{1,0:T(8,128)(2,1)} %get-tuple-element.10), channel_id=1, source_target_pairs={{16,0},{32,16},{48,32},{64,48},{80,64},{96,80},{112,96},{128,112},... | collective-permute-start | bytes 589832 | tf_op jit(solution)/shard_map/ppermute | solution.py:206
Sparse Core Ops, SparseCore 0:
  26.4 61.8 all-gather.2

commit v2 on v1

--- a/solution.py
+++ b/solution.py
@@ -10,6 +10,7 @@
 
 W = 8
 EARLY = 8
+AHEAD = 7
 LATE = 6
 
 
@@ -70,36 +71,47 @@
     return lax.rem(col_index - row_index * rows + W + groups * rows * 64, groups)
 
 
-def pack_kernel(rows, groups, table, pattern, keep, density, early, up, down):
+def masked_tile(pattern, density, slot):
+    safe = jnp.maximum(slot, 0)
+    used = (slot >= 0) & (pattern[lax.rem(safe, 2), safe // 2] == 1)
+    tile = density[safe]
+    return jnp.where(used, tile, jnp.zeros_like(tile))
+
+
+def halo_kernel(rows, groups, table, pattern, density, up, down):
     size = density.shape[-1]
     width = EARLY + 2 * LATE
     r = lax.axis_index("row")
     c = lax.axis_index("col")
-    own = relative(r, c, rows, groups)
     after = relative(r + 1, c, rows, groups)
     before = relative(r + lax.axis_size("row") - 1, c, rows, groups)
-
-    def move(target, e, slot):
-        safe = jnp.maximum(slot, 0)
-        used = (slot >= 0) & (pattern[safe // 2, lax.rem(safe, 2)] == 1)
-        tile = density[safe]
-        target[pl.ds(e * size, size), :] = jnp.where(used, tile, jnp.zeros_like(tile))
-
+    for e in range(LATE):
+        place = pl.ds(e * size, size)
+        up[place, :] = masked_tile(pattern, density, table[after * width + EARLY + e])
+        down[place, :] = masked_tile(pattern, density, table[before * width + EARLY + LATE + e])
+
+
+def own_kernel(rows, groups, table, pattern, keep, density, mine, extra, marks):
+    size = density.shape[-1]
+    width = EARLY + 2 * LATE
+    own = relative(lax.axis_index("row"), lax.axis_index("col"), rows, groups)
     for e in range(EARLY):
-        move(early, e, table[own * width + e])
-    for e in range(LATE):
-        move(up, e, table[after * width + EARLY + e])
-        move(down, e, table[before * width + EARLY + LATE + e])
+        target, place = (mine, e) if e < AHEAD else (extra, e - AHEAD)
+        target[pl.ds(place * size, size), :] = masked_tile(pattern, density, table[own * width + e])
     flags = jnp.zeros((32, size), jnp.float32)
     line = lax.broadcasted_iota(jnp.int32, (32, size), 0)
     for a in range(rows):
         for q in range(2):
-            value = jnp.where(keep[a, q] == 1, 1.0, 0.0)
+            value = jnp.where(keep[q, a] == 1, 1.0, 0.0)
             flags = jnp.where(line == a * 2 + q, value, flags)
-    early[pl.ds(EARLY * size, 32), :] = flags.astype(jnp.bfloat16)
-
-
-def multiply_kernel(rows, groups, early_tiles, late_tiles, keep, gathered, out, dense, square, columns, flags):
+    marks[...] = flags.astype(jnp.bfloat16)
+
+
+def multiply_kernel(rows, groups, early_tiles, late_tiles, keep, *refs):
+    reach = groups // 4 - 1
+    own_early, own_late = refs[:2]
+    early_got, late_got = refs[2 : 2 + reach], refs[2 + reach : 2 + 2 * reach]
+    far, out, pieces, dense, square, columns, flags, sems = refs[2 + 2 * reach :]
     size = out.shape[-1]
     window = rows + 2 * W
     r = lax.axis_index("row")
@@ -110,20 +122,47 @@
     half = W // 2
     supers = window // 2
 
+    chips = groups // 2
+    core = lax.rem(c, 2)
+    first_lines = AHEAD * size
+    last_lines = (EARLY - AHEAD + LATE) * size + 32
+    copies = []
+    for o in range(chips):
+        for h in range(2):
+            if o == 0:
+                parts = [(own_early, h * first_lines), (own_late, h * last_lines)]
+            elif o == chips // 2:
+                base = h * (first_lines + last_lines)
+                parts = [(far, base), (far, base + first_lines)]
+            else:
+                s = min(o, chips - o) - 1
+                part = h + (2 if o < chips // 2 else 0)
+                parts = [(early_got[s], part * first_lines), (late_got[s], part * last_lines)]
+            place = 2 * o + h
+            for k, (source, line) in enumerate(parts):
+                start, count = ((0, first_lines), (first_lines, last_lines))[k]
+                copy = pltpu.make_async_copy(
+                    source.at[pl.ds(line, count), :], pieces.at[place, pl.ds(start, count), :], sems.at[place, k]
+                )
+                copy.start()
+                copies.append(copy)
+
     nothing = jnp.zeros((size, size), jnp.bfloat16)
     for u in range(window):
         for v in range(window):
             if abs(u - v) > W and abs(u // 2 - v // 2) <= half:
                 dense[pl.ds(u * size, size), pl.ds(v * size, size)] = nothing
+    for copy in copies:
+        copy.wait()
     for n in range(groups):
-        p = lax.rem(turn + n, groups)
+        place = lax.rem(turn + n + groups - (c - core), groups)
         for e, (w, j) in enumerate(early_tiles[n] + late_tiles[n]):
-            line = e * size if e < len(early_tiles[n]) else (EARLY + e - len(early_tiles[n])) * size + 32
-            tile = gathered[p, pl.ds(line, size), :]
+            line = (e if e < len(early_tiles[n]) else EARLY + e - len(early_tiles[n])) * size
+            tile = pieces[place, pl.ds(line, size), :]
             dense[pl.ds(w * size, size), pl.ds(j * size, size)] = tile
             if w != j:
                 dense[pl.ds(j * size, size), pl.ds(w * size, size)] = tile.T
-        flags[pl.ds(n * 32, 32), :] = gathered[p, pl.ds(EARLY * size, 32), :].astype(jnp.float32)
+        flags[pl.ds(n * 32, 32), :] = pieces[place, pl.ds((EARLY + LATE) * size, 32), :].astype(jnp.float32)
 
     first = pl.multiple_of(m * size, size)
     second = pl.multiple_of(jnp.minimum(m + groups, window - 1) * size, size)
@@ -140,6 +179,8 @@
         top = half + step
         line = top * pair
         for other in range(top - half, top + half + 1):
+            if half <= other < top:
+                continue
             low = max(top, other) - half
             high = min(top, other) + half + 1
             product = jnp.dot(
@@ -158,6 +199,8 @@
                         tile = product[x * size : (x + 1) * size, y * size : (y + 1) * size]
                         tile = jnp.where(flag > 0.5, tile, 0.0).astype(jnp.bfloat16)
                     square[pl.ds(a * size, size), pl.ds(k * size, size)] = tile
+                    if top < other < half + rows // 2:
+                        square[pl.ds((k - W) * size, size), pl.ds((a + W) * size, size)] = tile.T
         low = (top - half) * pair
         deep = (2 * half + 1) * pair
         cubic = jnp.dot(
@@ -174,8 +217,8 @@
             chosen = jnp.where(upper, third[:, :size], third[:, size:])
             base = square[pl.ds(a * size, size), pl.ds(start, size)].astype(jnp.float32)
             value = 3.0 * base - 2.0 * chosen
-            out[2 * a] = jnp.where(keep[a, 0] == 1, value, 0.0).astype(out.dtype)
-            there = (keep[a, 1] == 1) & (a == m)
+            out[2 * a] = jnp.where(keep[0, a] == 1, value, 0.0).astype(out.dtype)
+            there = (keep[1, a] == 1) & (a == m)
             base = square[pl.ds(a * size, size), pl.ds(second, size)].astype(jnp.float32)
             value = 3.0 * base - 2.0 * third[:, size:]
             out[2 * a + 1] = jnp.where(there, value, 0.0).astype(out.dtype)
@@ -190,36 +233,77 @@
     window = rows + 2 * W
     smem = pl.BlockSpec(memory_space=pltpu.SMEM)
     vmem = pl.BlockSpec(memory_space=pltpu.VMEM)
-    early, up, down = pl.pallas_call(
-        functools.partial(pack_kernel, rows, groups),
+    space = pl.BlockSpec(memory_space=pl.ANY)
+    tiles = density.reshape(rows * slots, size, size)
+    pattern, keep = density_pattern.T, filter_pattern.T
+    lines = (EARLY + LATE) * size + 32
+    part = jax.ShapeDtypeStruct((LATE * size, size), jnp.bfloat16)
+    early, extra, marks = pl.pallas_call(
+        functools.partial(own_kernel, rows, groups),
         out_shape=[
-            jax.ShapeDtypeStruct((EARLY * size + 32, size), jnp.bfloat16),
-            jax.ShapeDtypeStruct((LATE * size, size), jnp.bfloat16),
-            jax.ShapeDtypeStruct((LATE * size, size), jnp.bfloat16),
+            jax.ShapeDtypeStruct((AHEAD * size, size), jnp.bfloat16),
+            jax.ShapeDtypeStruct(((EARLY - AHEAD) * size, size), jnp.bfloat16),
+            jax.ShapeDtypeStruct((32, size), jnp.bfloat16),
         ],
         in_specs=[smem, smem, smem, vmem],
         out_specs=[vmem, vmem, vmem],
-        name="pack",
-    )(table, density_pattern, filter_pattern, density.reshape(rows * slots, size, size))
+        name="own_tiles",
+    )(table, pattern, keep, tiles)
     forward = [(i, (i + 1) % count) for i in range(count)]
     backward = [(j, i) for i, j in forward]
+    chips = groups // 2
+    ring = [(2 * z, 2 * ((z + 1) % chips)) for z in range(chips)]
+    ring += [(2 * z + 1, 2 * ((z - 1) % chips) + 1) for z in range(chips)]
+    mates = [(i, i ^ 1) for i in range(groups)]
+    both = [[2 * z, 2 * z + 1] for z in range(chips)]
+    core = lax.rem(lax.axis_index("col"), 2)
+
+    def with_mate(value):
+        return lax.all_gather(value, "col", axis=0, tiled=True, axis_index_groups=both)
+
+    def half(value):
+        lines = value.shape[0] // 2
+        return lax.dynamic_slice_in_dim(value, core * lines, lines, axis=0)
+
+    own_early = with_mate(early)
+    tiles, own_early = lax.optimization_barrier((tiles, own_early))
+    up, down = pl.pallas_call(
+        functools.partial(halo_kernel, rows, groups),
+        out_shape=[part, part],
+        in_specs=[smem, smem, vmem],
+        out_specs=[vmem, vmem],
+        name="halo_tiles",
+    )(table, pattern, tiles)
+    early_got = [lax.ppermute(own_early, "col", ring)]
     late = lax.ppermute(up, "row", forward) + lax.ppermute(down, "row", backward)
-    mine = jnp.concatenate([early, late], axis=0)
-    gathered = lax.all_gather(mine, "col", axis=0, tiled=False)
+    late = jnp.concatenate([extra, late, marks], axis=0)
+    late, early_got[0] = lax.optimization_barrier((late, early_got[0]))
+    own_late = with_mate(late)
+    late_got = [lax.ppermute(own_late, "col", ring)]
+    for _ in range(chips // 2 - 2):
+        early_got.append(lax.ppermute(early_got[-1], "col", ring))
+        late_got.append(lax.ppermute(late_got[-1], "col", ring))
+    early_last = lax.ppermute(half(early_got[-1]), "col", ring)
+    late_last = lax.ppermute(half(late_got[-1]), "col", ring)
+    early_got = [with_mate(value) for value in early_got]
+    late_got = [with_mate(value) for value in late_got]
+    far = with_mate(jnp.concatenate([early_last, late_last], axis=0))
     out = pl.pallas_call(
         functools.partial(multiply_kernel, rows, groups, early_tiles, late_tiles),
         out_shape=jax.ShapeDtypeStruct((rows * slots, size, size), jnp.bfloat16),
-        in_specs=[smem, vmem],
+        in_specs=[smem] + [space] * (3 + len(early_got) + len(late_got)),
         out_specs=vmem,
         scratch_shapes=[
+            pltpu.VMEM((groups, lines, size), jnp.bfloat16),
             pltpu.VMEM((window * size, window * size), jnp.bfloat16),
             pltpu.VMEM((rows * size, window * size), jnp.bfloat16),
             pltpu.VMEM((window * size, 2 * size), jnp.bfloat16),
             pltpu.VMEM((groups * 32, size), jnp.float32),
+            pltpu.SemaphoreType.DMA((groups, 2)),
         ],
         compiler_params=pltpu.CompilerParams(vmem_limit_bytes=60 * 1024 * 1024),
         name="multiply",
-    )(filter_pattern, gathered)
+    )(keep, own_early, own_late, *early_got, *late_got, far)
     return out.reshape(rows, slots, size, size)
 
 

time: 117 us -> 104 us (0.89); the launches traced: 117 us -> 102 us
  waiting for transfers between devices: 65 us -> 6.74 us
  blocking collectives: 0 us -> 32.1 us
  starting transfers between devices: 10 us -> 38.8 us
  between operations: 13.4 us -> 0.33 us
  local copies, waits for them, and re-layouts: 2.7 us -> 0.67 us
  other arithmetic: 1.81 us -> 0.1 us
    all_gather x1 -> x0, waiting for transfers between devices: 62 us -> none  [per_device(): gathered = lax.all_gather(mine, 'col', axis=0, tiled=False)]
    all_gather x0 -> x9, blocking collectives: none -> 32.1 us  [with_mate(): lax.all_gather(value, 'col', axis=0, tiled=True, axis_index_groups=both)]
    ppermute x0 -> x8, starting transfers between devices: none -> 29.6 us  [the longest x2 8.19 us: per_device(): late_got.append(lax.ppermute(late_got[-1], 'col', ring))]
    ppermute x0 -> x8, waiting for transfers between devices: none -> 3.83 us  [the longest x1 3.4 us: per_device(): late_got = [lax.ppermute(own_late, 'col', ring)]]
    pallas_call x1, Pallas kernels: 22 us -> 19.4 us  [per_device(): pl.pallas_call(functools.partial(multiply_kernel, rows, groups, early_til...]
    unnamed x2 -> x8, local copies, waits for them, and re-layouts: 2.7 us -> 0.63 us
    pallas_call x1 -> x2, Pallas kernels: 2.23 us -> 3.99 us  [the longest x1 2.03 us: per_device(): pl.pallas_call(functools.partial(halo_kernel, rows, groups), out_shape=[p...]
    concatenate x1 -> x2, other arithmetic: 1.75 us -> 0.05 us  [the longest x1 0.03 us: per_device(): far = with_mate(jnp.concatenate([early_last, late_last], axis=0))]
  transfers between devices with their start and end apart: 3 -> 10, of which waited for: 3 -> 4; matrix products, arithmetic and copies ran while one was open for 0% -> 0% of each run, Pallas kernels for 0% -> 2%
where the time goes in v2:
time: 104 us; the launch traced here: 102 us
  starting transfers between devices  38.8 us (37%)
  blocking collectives  32.1 us (31%)
  Pallas kernels  23.4 us (22%)
  waiting for transfers between devices  6.74 us (6%)
    all_gather x9, blocking collectives, with_mate(): lax.all_gather(value, 'col', axis=0, tiled=True, axis_index_groups=both)  32.1 us
    pallas_call x1, Pallas kernels, per_device(): pl.pallas_call(functools.partial(multiply_kernel, rows, groups, early_til...  19.4 us
    ppermute x2, starting transfers between devices, per_device(): late_got.append(lax.ppermute(late_got[-1], 'col', ring))  8.19 us
    ppermute x1, starting transfers between devices, per_device(): lax.ppermute(down, 'row', backward)  6.09 us
    ppermute x2, starting transfers between devices, per_device(): early_got.append(lax.ppermute(early_got[-1], 'col', ring))  5.48 us
    ppermute x1, starting transfers between devices, per_device(): early_got = [lax.ppermute(own_early, 'col', ring)]  5.28 us
    ppermute x1, starting transfers between devices, per_device(): late_got = [lax.ppermute(own_late, 'col', ring)]  4.33 us
    ppermute x1, starting transfers between devices, per_device(): late_last = lax.ppermute(half(late_got[-1]), 'col', ring)  3.98 us
  transfers between devices with their start and end apart: 10, of which 4 were waited for; matrix products, arithmetic and copies ran while one was open for 0% of the time, Pallas kernels for 2%

profile of v2, /device:TPU:1, one launch (start us, length us, event | category | flops | bytes accessed | tf_op | source)
XLA Modules:
  0.0 102.2 jit_solution(7708927307776148570)
XLA Ops:
  0.0 2.0 %own_tiles.1 = (bf16[896,128]{1,0:T(8,128)(2,1)}, bf16[128,128]{1,0:T(8,128)(2,1)}, bf16[32,128]{1,0:T(8,128)(2,1)}) custom-call(s32[320]{0:T(512)} %constant.20.clone.table, s32[2,12]{1,0:T(2,128)} %bitcast.6, s32[2,12]{1,0:T(2,128)} %bitcast.8, bf16[24,128,128]{2,1,0:T(8,128)(2,1)} %bitcast.4), custom_call_target="tpu_custom_call" | custom-call | tf_op jit(solution)/shard_map/own_tiles/pallas_call | solution.py:241
  2.0 8.8 %all_gather.27.refs_0_ = bf16[1792,128]{1,0:T(8,128)(2,1)S(1)} all-gather(bf16[896,128]{1,0:T(8,128)(2,1)} %get-tuple-element.14), channel_id=1, replica_groups={{0,1},{2,3},{4,5},{6,7},{8,9},{10,11},{12,13},{14,15},{16,17},{18,19},{..., dimensions={0}, use_global_device_ids=true | all-gather | bytes 688128 | tf_op jit(solution)/shard_map/all_gather | solution.py:262
  10.8 0.0 copy-start.1
  10.8 5.3 %collective-permute-start.2 = (bf16[1792,128]{1,0:T(8,128)(2,1)S(1)}, bf16[1792,128]{1,0:T(8,128)(2,1)S(1)}, u32[]{:S(2)}, u32[]{:S(2)}) collective-permute-start(bf16[1792,128]{1,0:T(8,128)(2,1)S(1)} %all_gather.27.refs_0_), channel_id=1, source_target_pairs={{0,2},{2,4},{4,6},{6,8},{8,10},{10,12},{12,14},{14,0},{1,15},{3,1}... | collective-permute-start | bytes 1376264 | tf_op jit(solution)/shard_map/ppermute | solution.py:277
  16.1 2.0 %halo_tiles.1 = (bf16[768,128]{1,0:T(8,128)(2,1)}, bf16[768,128]{1,0:T(8,128)(2,1)}) custom-call(s32[320]{0:T(512)} %constant.20.clone.table, s32[2,12]{1,0:T(2,128)} %bitcast.7, bf16[24,128,128]{2,1,0:T(8,128)(2,1)} %bitcast.5), custom_call_target="tpu_custom_call" | custom-call | tf_op jit(solution)/shard_map/halo_tiles/pallas_call | solution.py:270
  18.1 3.1 %collective-permute-start = (bf16[768,128]{1,0:T(8,128)(2,1)}, bf16[768,128]{1,0:T(8,128)(2,1)S(1)}, u32[]{:S(2)}, u32[]{:S(2)}) collective-permute-start(bf16[768,128]{1,0:T(8,128)(2,1)} %get-tuple-element.18), channel_id=1, source_target_pairs={{0,16},{16,32},{32,48},{48,64},{64,80},{80,96},{96,112},{112,128},... | collective-permute-start | bytes 589832 | tf_op jit(solution)/shard_map/ppermute | solution.py:278
  21.2 0.0 copy-start.2
  21.3 6.1 %collective-permute-start.1 = (bf16[768,128]{1,0:T(8,128)(2,1)}, bf16[768,128]{1,0:T(8,128)(2,1)S(1)}, u32[]{:S(2)}, u32[]{:S(2)}) collective-permute-start(bf16[768,128]{1,0:T(8,128)(2,1)} %get-tuple-element.19), channel_id=1, source_target_pairs={{16,0},{32,16},{48,32},{64,48},{80,64},{96,80},{112,96},{128,112},... | collective-permute-start | bytes 589832 | tf_op jit(solution)/shard_map/ppermute | solution.py:278
  27.4 1.3 %collective-permute-done = bf16[768,128]{1,0:T(8,128)(2,1)S(1)} collective-permute-done((bf16[768,128]{1,0:T(8,128)(2,1)}, bf16[768,128]{1,0:T(8,128)(2,1)S(1)}, u32[]{:S(2)}, u32[]{:S(2)}) %collective-permute-start) | collective-permute-done | bytes 196640 | tf_op jit(solution)/shard_map/ppermute | solution.py:278
  28.7 1.6 %collective-permute-done.1 = bf16[768,128]{1,0:T(8,128)(2,1)S(1)} collective-permute-done((bf16[768,128]{1,0:T(8,128)(2,1)}, bf16[768,128]{1,0:T(8,128)(2,1)S(1)}, u32[]{:S(2)}, u32[]{:S(2)}) %collective-permute-start.1) | collective-permute-done | bytes 196640 | tf_op jit(solution)/shard_map/ppermute | solution.py:278
  30.3 0.0 copy-start.3
  30.3 0.1 add.9
  30.3 0.0 copy-done.1
  30.3 0.0 copy-done.2
  30.3 0.6 copy-done.3
  31.0 0.0 collective-permute-done.2
  31.0 2.1 %all_gather.28.refs_1_ = bf16[1856,128]{1,0:T(8,128)(2,1)S(1)} all-gather(bf16[928,128]{1,0:T(8,128)(2,1)S(1)} %pad_maximum_fusion.1), channel_id=1, replica_groups={{0,1},{2,3},{4,5},{6,7},{8,9},{10,11},{12,13},{14,15},{16,17},{18,19},{..., dimensions={0}, use_global_device_ids=true | all-gather | bytes 712704 | tf_op jit(solution)/shard_map/all_gather | solution.py:262
  33.1 0.0 copy-start
  33.1 4.3 %collective-permute-start.5 = (bf16[1856,128]{1,0:T(8,128)(2,1)S(1)}, bf16[1856,128]{1,0:T(8,128)(2,1)S(1)}, u32[]{:S(2)}, u32[]{:S(2)}) collective-permute-start(bf16[1856,128]{1,0:T(8,128)(2,1)S(1)} %all_gather.28.refs_1_), channel_id=1, source_target_pairs={{0,2},{2,4},{4,6},{6,8},{8,10},{10,12},{12,14},{14,0},{1,15},{3,1}... | collective-permute-start | bytes 1425416 | tf_op jit(solution)/shard_map/ppermute | solution.py:282
  37.5 2.1 %collective-permute-start.3 = (bf16[1792,128]{1,0:T(8,128)(2,1)S(1)}, bf16[1792,128]{1,0:T(8,128)(2,1)S(1)}, u32[]{:S(2)}, u32[]{:S(2)}) collective-permute-start(bf16[1792,128]{1,0:T(8,128)(2,1)S(1)} %collective-permute-done.2), channel_id=1, source_target_pairs={{0,2},{2,4},{4,6},{6,8},{8,10},{10,12},{12,14},{14,0},{1,15},{3,1}... | collective-permute-start | bytes 1376264 | tf_op jit(solution)/shard_map/ppermute | solution.py:284
  39.6 3.4 %collective-permute-done.5 = bf16[1856,128]{1,0:T(8,128)(2,1)S(1)} collective-permute-done((bf16[1856,128]{1,0:T(8,128)(2,1)S(1)}, bf16[1856,128]{1,0:T(8,128)(2,1)S(1)}, u32[]{:S(2)}, u32[]{:S(2)}) %collective-permute-start.5) | collective-permute-done | bytes 475168 | tf_op jit(solution)/shard_map/ppermute | solution.py:282
  43.1 5.0 %collective-permute-start.6 = (bf16[1856,128]{1,0:T(8,128)(2,1)S(1)}, bf16[1856,128]{1,0:T(8,128)(2,1)S(1)}, u32[]{:S(2)}, u32[]{:S(2)}) collective-permute-start(bf16[1856,128]{1,0:T(8,128)(2,1)S(1)} %collective-permute-done.5), channel_id=1, source_target_pairs={{0,2},{2,4},{4,6},{6,8},{8,10},{10,12},{12,14},{14,0},{1,15},{3,1}... | collective-permute-start | bytes 1425416 | tf_op jit(solution)/shard_map/ppermute | solution.py:285
  48.1 2.6 %all_gather.29.refs_2_ = bf16[3584,128]{1,0:T(8,128)(2,1)} all-gather(bf16[1792,128]{1,0:T(8,128)(2,1)S(1)} %collective-permute-done.2), channel_id=1, replica_groups={{0,1},{2,3},{4,5},{6,7},{8,9},{10,11},{12,13},{14,15},{16,17},{18,19},{..., dimensions={0}, use_global_device_ids=true | all-gather | bytes 1376256 | tf_op jit(solution)/shard_map/all_gather | solution.py:262
  50.7 0.0 copy-done
  50.7 0.0 collective-permute-done.3
  50.7 3.3 %collective-permute-start.4 = (bf16[1792,128]{1,0:T(8,128)(2,1)S(1)}, bf16[1792,128]{1,0:T(8,128)(2,1)S(1)}, u32[]{:S(2)}, u32[]{:S(2)}) collective-permute-start(bf16[1792,128]{1,0:T(8,128)(2,1)S(1)} %collective-permute-done.3), channel_id=1, source_target_pairs={{0,2},{2,4},{4,6},{6,8},{8,10},{10,12},{12,14},{14,0},{1,15},{3,1}... | collective-permute-start | bytes 1376264 | tf_op jit(solution)/shard_map/ppermute | solution.py:284
  54.0 2.6 %all_gather.30.refs_3_ = bf16[3584,128]{1,0:T(8,128)(2,1)} all-gather(bf16[1792,128]{1,0:T(8,128)(2,1)S(1)} %collective-permute-done.3), channel_id=1, replica_groups={{0,1},{2,3},{4,5},{6,7},{8,9},{10,11},{12,13},{14,15},{16,17},{18,19},{..., dimensions={0}, use_global_device_ids=true | all-gather | bytes 1376256 | tf_op jit(solution)/shard_map/all_gather | solution.py:262
  56.6 2.6 %all_gather.32.refs_5_ = bf16[3712,128]{1,0:T(8,128)(2,1)} all-gather(bf16[1856,128]{1,0:T(8,128)(2,1)S(1)} %collective-permute-done.5), channel_id=1, replica_groups={{0,1},{2,3},{4,5},{6,7},{8,9},{10,11},{12,13},{14,15},{16,17},{18,19},{..., dimensions={0}, use_global_device_ids=true | all-gather | bytes 1425408 | tf_op jit(solution)/shard_map/all_gather | solution.py:262
  59.2 0.0 collective-permute-done.6
  59.2 3.2 %collective-permute-start.7 = (bf16[1856,128]{1,0:T(8,128)(2,1)S(1)}, bf16[1856,128]{1,0:T(8,128)(2,1)S(1)}, u32[]{:S(2)}, u32[]{:S(2)}) collective-permute-start(bf16[1856,128]{1,0:T(8,128)(2,1)S(1)} %collective-permute-done.6), channel_id=1, source_target_pairs={{0,2},{2,4},{4,6},{6,8},{8,10},{10,12},{12,14},{14,0},{1,15},{3,1}... | collective-permute-start | bytes 1425416 | tf_op jit(solution)/shard_map/ppermute | solution.py:285
  62.4 0.0 collective-permute-done.4
  62.5 2.4 %collective-permute-start.8 = (bf16[896,128]{1,0:T(8,128)(2,1)S(1)}, bf16[896,128]{1,0:T(8,128)(2,1)S(1)}, u32[]{:S(2)}, u32[]{:S(2)}) collective-permute-start(bf16[896,128]{1,0:T(8,128)(2,1)S(1)} %constant_dynamic-slice_fusion.1), channel_id=1, source_target_pairs={{0,2},{2,4},{4,6},{6,8},{8,10},{10,12},{12,14},{14,0},{1,15},{3,1}... | collective-permute-start | bytes 688136 | tf_op jit(solution)/shard_map/ppermute | solution.py:286
  64.8 2.6 %all_gather.31.refs_4_ = bf16[3584,128]{1,0:T(8,128)(2,1)} all-gather(bf16[1792,128]{1,0:T(8,128)(2,1)S(1)} %collective-permute-done.4), channel_id=1, replica_groups={{0,1},{2,3},{4,5},{6,7},{8,9},{10,11},{12,13},{14,15},{16,17},{18,19},{..., dimensions={0}, use_global_device_ids=true | all-gather | bytes 1376256 | tf_op jit(solution)/shard_map/all_gather | solution.py:262
  67.4 2.6 %all_gather.33.refs_6_ = bf16[3712,128]{1,0:T(8,128)(2,1)} all-gather(bf16[1856,128]{1,0:T(8,128)(2,1)S(1)} %collective-permute-done.6), channel_id=1, replica_groups={{0,1},{2,3},{4,5},{6,7},{8,9},{10,11},{12,13},{14,15},{16,17},{18,19},{..., dimensions={0}, use_global_device_ids=true | all-gather | bytes 1425408 | tf_op jit(solution)/shard_map/all_gather | solution.py:262
  70.0 0.0 collective-permute-done.7
  70.1 4.0 %collective-permute-start.9 = (bf16[928,128]{1,0:T(8,128)(2,1)S(1)}, bf16[928,128]{1,0:T(8,128)(2,1)S(1)}, u32[]{:S(2)}, u32[]{:S(2)}) collective-permute-start(bf16[928,128]{1,0:T(8,128)(2,1)S(1)} %constant_dynamic-slice_fusion), channel_id=1, source_target_pairs={{0,2},{2,4},{4,6},{6,8},{8,10},{10,12},{12,14},{14,0},{1,15},{3,1}... | collective-permute-start | bytes 712712 | tf_op jit(solution)/shard_map/ppermute | solution.py:287
  74.0 2.6 %all_gather.34.refs_7_ = bf16[3712,128]{1,0:T(8,128)(2,1)} all-gather(bf16[1856,128]{1,0:T(8,128)(2,1)S(1)} %collective-permute-done.7), channel_id=1, replica_groups={{0,1},{2,3},{4,5},{6,7},{8,9},{10,11},{12,13},{14,15},{16,17},{18,19},{..., dimensions={0}, use_global_device_ids=true | all-gather | bytes 1425408 | tf_op jit(solution)/shard_map/all_gather | solution.py:262
  76.7 0.0 collective-permute-done.8
  76.7 0.4 collective-permute-done.9
  77.1 5.5 %all_gather.35.refs_8_ = bf16[3648,128]{1,0:T(8,128)(2,1)} all-gather(bf16[1824,128]{1,0:T(8,128)(2,1)S(1)} %pad_maximum_fusion), channel_id=1, replica_groups={{0,1},{2,3},{4,5},{6,7},{8,9},{10,11},{12,13},{14,15},{16,17},{18,19},{..., dimensions={0}, use_global_device_ids=true | all-gather | bytes 1400832 | tf_op jit(solution)/shard_map/all_gather | solution.py:262
  82.6 19.4 %multiply.1 = bf16[24,128,128]{2,1,0:T(8,128)(2,1)} custom-call(s32[2,12]{1,0:T(2,128)} %bitcast.9, bf16[1792,128]{1,0:T(8,128)(2,1)} %copy-done.1, bf16[1856,128]{1,0:T(8,128)(2,1)} %copy-done, bf16[3584,128]{1,0:T(8,128)(2,1)} %all_gather.29.refs_2_, bf16[3584,128]{1,0:T(8,128)(2,1)} %all_gather.30.refs_3_, bf16[3584,128]{1,0:T(8,128)(2,1)} %all_gather.31.refs_4_, ...), custom_call_target="tpu_custom_call" | custom-call | tf_op jit(solution)/shard_map/multiply/pallas_call | solution.py:291
  (4 shorter events, 0.1 us)
Async XLA Ops:
  10.8 19.5 %copy-start.1 = (bf16[1792,128]{1,0:T(8,128)(2,1)}, bf16[1792,128]{1,0:T(8,128)(2,1)S(1)}, u32[]{:S(2)}) copy-start(bf16[1792,128]{1,0:T(8,128)(2,1)S(1)} %all_gather.27.refs_0_) | copy-start | bytes 1376260
  10.8 20.2 %collective-permute-start.2 = (bf16[1792,128]{1,0:T(8,128)(2,1)S(1)}, bf16[1792,128]{1,0:T(8,128)(2,1)S(1)}, u32[]{:S(2)}, u32[]{:S(2)}) collective-permute-start(bf16[1792,128]{1,0:T(8,128)(2,1)S(1)} %all_gather.27.refs_0_), channel_id=1, source_target_pairs={{0,2},{2,4},{4,6},{6,8},{8,10},{10,12},{12,14},{14,0},{1,15},{3,1}... | collective-permute-start | bytes 1376264 | tf_op jit(solution)/shard_map/ppermute | solution.py:277
  18.1 10.5 %collective-permute-start = (bf16[768,128]{1,0:T(8,128)(2,1)}, bf16[768,128]{1,0:T(8,128)(2,1)S(1)}, u32[]{:S(2)}, u32[]{:S(2)}) collective-permute-start(bf16[768,128]{1,0:T(8,128)(2,1)} %get-tuple-element.18), channel_id=1, source_target_pairs={{0,16},{16,32},{32,48},{48,64},{64,80},{80,96},{96,112},{112,128},... | collective-permute-start | bytes 589832 | tf_op jit(solution)/shard_map/ppermute | solution.py:278
  21.2 9.1 %copy-start.2 = (bf16[128,128]{1,0:T(8,128)(2,1)S(1)}, bf16[128,128]{1,0:T(8,128)(2,1)}, u32[]{:S(2)}) copy-start(bf16[128,128]{1,0:T(8,128)(2,1)} %get-tuple-element.16) | copy-start | bytes 98308
  21.3 9.0 %collective-permute-start.1 = (bf16[768,128]{1,0:T(8,128)(2,1)}, bf16[768,128]{1,0:T(8,128)(2,1)S(1)}, u32[]{:S(2)}, u32[]{:S(2)}) collective-permute-start(bf16[768,128]{1,0:T(8,128)(2,1)} %get-tuple-element.19), channel_id=1, source_target_pairs={{16,0},{32,16},{48,32},{64,48},{80,64},{96,80},{112,96},{128,112},... | collective-permute-start | bytes 589832 | tf_op jit(solution)/shard_map/ppermute | solution.py:278
  30.3 0.7 copy-start.3
  33.1 17.5 %copy-start = (bf16[1856,128]{1,0:T(8,128)(2,1)}, bf16[1856,128]{1,0:T(8,128)(2,1)S(1)}, u32[]{:S(2)}) copy-start(bf16[1856,128]{1,0:T(8,128)(2,1)S(1)} %all_gather.28.refs_1_) | copy-start | bytes 1425412
  33.1 9.9 %collective-permute-start.5 = (bf16[1856,128]{1,0:T(8,128)(2,1)S(1)}, bf16[1856,128]{1,0:T(8,128)(2,1)S(1)}, u32[]{:S(2)}, u32[]{:S(2)}) collective-permute-start(bf16[1856,128]{1,0:T(8,128)(2,1)S(1)} %all_gather.28.refs_1_), channel_id=1, source_target_pairs={{0,2},{2,4},{4,6},{6,8},{8,10},{10,12},{12,14},{14,0},{1,15},{3,1}... | collective-permute-start | bytes 1425416 | tf_op jit(solution)/shard_map/ppermute | solution.py:282
  37.5 13.2 %collective-permute-start.3 = (bf16[1792,128]{1,0:T(8,128)(2,1)S(1)}, bf16[1792,128]{1,0:T(8,128)(2,1)S(1)}, u32[]{:S(2)}, u32[]{:S(2)}) collective-permute-start(bf16[1792,128]{1,0:T(8,128)(2,1)S(1)} %collective-permute-done.2), channel_id=1, source_target_pairs={{0,2},{2,4},{4,6},{6,8},{8,10},{10,12},{12,14},{14,0},{1,15},{3,1}... | collective-permute-start | bytes 1376264 | tf_op jit(solution)/shard_map/ppermute | solution.py:284
  43.1 16.2 %collective-permute-start.6 = (bf16[1856,128]{1,0:T(8,128)(2,1)S(1)}, bf16[1856,128]{1,0:T(8,128)(2,1)S(1)}, u32[]{:S(2)}, u32[]{:S(2)}) collective-permute-start(bf16[1856,128]{1,0:T(8,128)(2,1)S(1)} %collective-permute-done.5), channel_id=1, source_target_pairs={{0,2},{2,4},{4,6},{6,8},{8,10},{10,12},{12,14},{14,0},{1,15},{3,1}... | collective-permute-start | bytes 1425416 | tf_op jit(solution)/shard_map/ppermute | solution.py:285
  50.7 11.7 %collective-permute-start.4 = (bf16[1792,128]{1,0:T(8,128)(2,1)S(1)}, bf16[1792,128]{1,0:T(8,128)(2,1)S(1)}, u32[]{:S(2)}, u32[]{:S(2)}) collective-permute-start(bf16[1792,128]{1,0:T(8,128)(2,1)S(1)} %collective-permute-done.3), channel_id=1, source_target_pairs={{0,2},{2,4},{4,6},{6,8},{8,10},{10,12},{12,14},{14,0},{1,15},{3,1}... | collective-permute-start | bytes 1376264 | tf_op jit(solution)/shard_map/ppermute | solution.py:284
  59.2 10.8 %collective-permute-start.7 = (bf16[1856,128]{1,0:T(8,128)(2,1)S(1)}, bf16[1856,128]{1,0:T(8,128)(2,1)S(1)}, u32[]{:S(2)}, u32[]{:S(2)}) collective-permute-start(bf16[1856,128]{1,0:T(8,128)(2,1)S(1)} %collective-permute-done.6), channel_id=1, source_target_pairs={{0,2},{2,4},{4,6},{6,8},{8,10},{10,12},{12,14},{14,0},{1,15},{3,1}... | collective-permute-start | bytes 1425416 | tf_op jit(solution)/shard_map/ppermute | solution.py:285
  62.5 14.2 %collective-permute-start.8 = (bf16[896,128]{1,0:T(8,128)(2,1)S(1)}, bf16[896,128]{1,0:T(8,128)(2,1)S(1)}, u32[]{:S(2)}, u32[]{:S(2)}) collective-permute-start(bf16[896,128]{1,0:T(8,128)(2,1)S(1)} %constant_dynamic-slice_fusion.1), channel_id=1, source_target_pairs={{0,2},{2,4},{4,6},{6,8},{8,10},{10,12},{12,14},{14,0},{1,15},{3,1}... | collective-permute-start | bytes 688136 | tf_op jit(solution)/shard_map/ppermute | solution.py:286
  70.1 7.0 %collective-permute-start.9 = (bf16[928,128]{1,0:T(8,128)(2,1)S(1)}, bf16[928,128]{1,0:T(8,128)(2,1)S(1)}, u32[]{:S(2)}, u32[]{:S(2)}) collective-permute-start(bf16[928,128]{1,0:T(8,128)(2,1)S(1)} %constant_dynamic-slice_fusion), channel_id=1, source_target_pairs={{0,2},{2,4},{4,6},{6,8},{8,10},{10,12},{12,14},{14,0},{1,15},{3,1}... | collective-permute-start | bytes 712712 | tf_op jit(solution)/shard_map/ppermute | solution.py:287

commit v3 on v2

--- a/solution.py
+++ b/solution.py
@@ -111,7 +111,7 @@
     reach = groups // 4 - 1
     own_early, own_late = refs[:2]
     early_got, late_got = refs[2 : 2 + reach], refs[2 + reach : 2 + 2 * reach]
-    far, out, pieces, dense, square, columns, flags, sems = refs[2 + 2 * reach :]
+    far_early, far_late, out, pieces, dense, square, columns, flags, sems = refs[2 + 2 * reach :]
     size = out.shape[-1]
     window = rows + 2 * W
     r = lax.axis_index("row")
@@ -120,7 +120,6 @@
     turn = lax.rem(c - m + groups, groups)
     pair = 2 * size
     half = W // 2
-    supers = window // 2
 
     chips = groups // 2
     core = lax.rem(c, 2)
@@ -132,8 +131,7 @@
             if o == 0:
                 parts = [(own_early, h * first_lines), (own_late, h * last_lines)]
             elif o == chips // 2:
-                base = h * (first_lines + last_lines)
-                parts = [(far, base), (far, base + first_lines)]
+                parts = [(far_early, h * first_lines), (far_late, h * last_lines)]
             else:
                 s = min(o, chips - o) - 1
                 part = h + (2 if o < chips // 2 else 0)
@@ -287,11 +285,11 @@
     late_last = lax.ppermute(half(late_got[-1]), "col", ring)
     early_got = [with_mate(value) for value in early_got]
     late_got = [with_mate(value) for value in late_got]
-    far = with_mate(jnp.concatenate([early_last, late_last], axis=0))
+    far = [with_mate(early_last), with_mate(late_last)]
     out = pl.pallas_call(
         functools.partial(multiply_kernel, rows, groups, early_tiles, late_tiles),
         out_shape=jax.ShapeDtypeStruct((rows * slots, size, size), jnp.bfloat16),
-        in_specs=[smem] + [space] * (3 + len(early_got) + len(late_got)),
+        in_specs=[smem] + [space] * (4 + len(early_got) + len(late_got)),
         out_specs=vmem,
         scratch_shapes=[
             pltpu.VMEM((groups, lines, size), jnp.bfloat16),
@@ -303,7 +301,7 @@
         ],
         compiler_params=pltpu.CompilerParams(vmem_limit_bytes=60 * 1024 * 1024),
         name="multiply",
-    )(keep, own_early, own_late, *early_got, *late_got, far)
+    )(keep, own_early, own_late, *early_got, *late_got, *far)
     return out.reshape(rows, slots, size, size)
 
 

time: 104 us -> 111 us (1.067)
  blocking collectives: 32.1 us -> 34.8 us
  waiting for transfers between devices: 6.74 us -> 9.06 us
  starting transfers between devices: 38.8 us -> 40.7 us
    ppermute x2, waiting for transfers between devices: 0.01 us -> 5.72 us  [per_device(): early_got.append(lax.ppermute(early_got[-1], 'col', ring))]
    ppermute x1, waiting for transfers between devices: 3.4 us -> 0.01 us  [per_device(): late_got = [lax.ppermute(own_late, 'col', ring)]]
    all_gather x9 -> x10, blocking collectives: 32.1 us -> 34.8 us  [with_mate(): lax.all_gather(value, 'col', axis=0, tiled=True, axis_index_groups=both)]
    ppermute x2, starting transfers between devices: 5.48 us -> 7.16 us  [per_device(): early_got.append(lax.ppermute(early_got[-1], 'col', ring))]
    ppermute x2, starting transfers between devices: 8.19 us -> 6.9 us  [per_device(): late_got.append(lax.ppermute(late_got[-1], 'col', ring))]
where the time goes in v3:
time: 111 us; the launch traced here: 109 us
  starting transfers between devices  40.7 us (37%)
  blocking collectives  34.8 us (31%)
  Pallas kernels  23.4 us (21%)
  waiting for transfers between devices  9.06 us (8%)
    all_gather x10, blocking collectives, with_mate(): lax.all_gather(value, 'col', axis=0, tiled=True, axis_index_groups=both)  34.8 us
    pallas_call x1, Pallas kernels, per_device(): pl.pallas_call(functools.partial(multiply_kernel, rows, groups, early_til...  19.4 us
    ppermute x2, starting transfers between devices, per_device(): early_got.append(lax.ppermute(early_got[-1], 'col', ring))  7.16 us
    ppermute x2, starting transfers between devices, per_device(): late_got.append(lax.ppermute(late_got[-1], 'col', ring))  6.9 us
    ppermute x1, starting transfers between devices, per_device(): lax.ppermute(down, 'row', backward)  6.09 us
    ppermute x2, waiting for transfers between devices, per_device(): early_got.append(lax.ppermute(early_got[-1], 'col', ring))  5.72 us
    ppermute x1, starting transfers between devices, per_device(): early_got = [lax.ppermute(own_early, 'col', ring)]  5.28 us
    ppermute x1, starting transfers between devices, per_device(): late_last = lax.ppermute(half(late_got[-1]), 'col', ring)  4.49 us
  transfers between devices with their start and end apart: 10, of which 4 were waited for; matrix products, arithmetic and copies ran while one was open for 0% of the time, Pallas kernels for 2%

profile of v3, /device:TPU:1, one launch (start us, length us, event | category | flops | bytes accessed | tf_op | source)
XLA Modules:
  0.0 109.0 jit_solution(700772630904119928)
XLA Ops:
  0.0 2.0 %own_tiles.1 = (bf16[896,128]{1,0:T(8,128)(2,1)}, bf16[128,128]{1,0:T(8,128)(2,1)}, bf16[32,128]{1,0:T(8,128)(2,1)}) custom-call(s32[320]{0:T(512)} %constant.20.clone.table, s32[2,12]{1,0:T(2,128)} %bitcast.6, s32[2,12]{1,0:T(2,128)} %bitcast.8, bf16[24,128,128]{2,1,0:T(8,128)(2,1)} %bitcast.4), custom_call_target="tpu_custom_call" | custom-call | tf_op jit(solution)/shard_map/own_tiles/pallas_call | solution.py:239
  2.0 8.8 %all_gather.30.refs_0_ = bf16[1792,128]{1,0:T(8,128)(2,1)S(1)} all-gather(bf16[896,128]{1,0:T(8,128)(2,1)} %get-tuple-element.14), channel_id=1, replica_groups={{0,1},{2,3},{4,5},{6,7},{8,9},{10,11},{12,13},{14,15},{16,17},{18,19},{..., dimensions={0}, use_global_device_ids=true | all-gather | bytes 688128 | tf_op jit(solution)/shard_map/all_gather | solution.py:260
  10.8 0.0 copy-start.1
  10.8 5.3 %collective-permute-start.2 = (bf16[1792,128]{1,0:T(8,128)(2,1)S(1)}, bf16[1792,128]{1,0:T(8,128)(2,1)S(1)}, u32[]{:S(2)}, u32[]{:S(2)}) collective-permute-start(bf16[1792,128]{1,0:T(8,128)(2,1)S(1)} %all_gather.30.refs_0_), channel_id=1, source_target_pairs={{0,2},{2,4},{4,6},{6,8},{8,10},{10,12},{12,14},{14,0},{1,15},{3,1}... | collective-permute-start | bytes 1376264 | tf_op jit(solution)/shard_map/ppermute | solution.py:275
  16.1 2.0 %halo_tiles.1 = (bf16[768,128]{1,0:T(8,128)(2,1)}, bf16[768,128]{1,0:T(8,128)(2,1)}) custom-call(s32[320]{0:T(512)} %constant.20.clone.table, s32[2,12]{1,0:T(2,128)} %bitcast.7, bf16[24,128,128]{2,1,0:T(8,128)(2,1)} %bitcast.5), custom_call_target="tpu_custom_call" | custom-call | tf_op jit(solution)/shard_map/halo_tiles/pallas_call | solution.py:268
  18.1 3.1 %collective-permute-start = (bf16[768,128]{1,0:T(8,128)(2,1)}, bf16[768,128]{1,0:T(8,128)(2,1)S(1)}, u32[]{:S(2)}, u32[]{:S(2)}) collective-permute-start(bf16[768,128]{1,0:T(8,128)(2,1)} %get-tuple-element.18), channel_id=1, source_target_pairs={{0,16},{16,32},{32,48},{48,64},{64,80},{80,96},{96,112},{112,128},... | collective-permute-start | bytes 589832 | tf_op jit(solution)/shard_map/ppermute | solution.py:276
  21.2 0.0 copy-start.2
  21.3 6.1 %collective-permute-start.1 = (bf16[768,128]{1,0:T(8,128)(2,1)}, bf16[768,128]{1,0:T(8,128)(2,1)S(1)}, u32[]{:S(2)}, u32[]{:S(2)}) collective-permute-start(bf16[768,128]{1,0:T(8,128)(2,1)} %get-tuple-element.19), channel_id=1, source_target_pairs={{16,0},{32,16},{48,32},{64,48},{80,64},{96,80},{112,96},{128,112},... | collective-permute-start | bytes 589832 | tf_op jit(solution)/shard_map/ppermute | solution.py:276
  27.4 1.3 %collective-permute-done = bf16[768,128]{1,0:T(8,128)(2,1)S(1)} collective-permute-done((bf16[768,128]{1,0:T(8,128)(2,1)}, bf16[768,128]{1,0:T(8,128)(2,1)S(1)}, u32[]{:S(2)}, u32[]{:S(2)}) %collective-permute-start) | collective-permute-done | bytes 196640 | tf_op jit(solution)/shard_map/ppermute | solution.py:276
  28.7 1.6 %collective-permute-done.1 = bf16[768,128]{1,0:T(8,128)(2,1)S(1)} collective-permute-done((bf16[768,128]{1,0:T(8,128)(2,1)}, bf16[768,128]{1,0:T(8,128)(2,1)S(1)}, u32[]{:S(2)}, u32[]{:S(2)}) %collective-permute-start.1) | collective-permute-done | bytes 196640 | tf_op jit(solution)/shard_map/ppermute | solution.py:276
  30.3 0.0 copy-start.3
  30.3 0.1 add.9
  30.3 0.0 copy-done.1
  30.3 0.0 copy-done.2
  30.3 0.6 copy-done.3
  31.0 0.0 collective-permute-done.2
  31.0 2.1 %all_gather.31.refs_1_ = bf16[1856,128]{1,0:T(8,128)(2,1)S(1)} all-gather(bf16[928,128]{1,0:T(8,128)(2,1)S(1)} %pad_maximum_fusion), channel_id=1, replica_groups={{0,1},{2,3},{4,5},{6,7},{8,9},{10,11},{12,13},{14,15},{16,17},{18,19},{..., dimensions={0}, use_global_device_ids=true | all-gather | bytes 712704 | tf_op jit(solution)/shard_map/all_gather | solution.py:260
  33.1 0.0 copy-start
  33.1 4.3 %collective-permute-start.5 = (bf16[1856,128]{1,0:T(8,128)(2,1)S(1)}, bf16[1856,128]{1,0:T(8,128)(2,1)S(1)}, u32[]{:S(2)}, u32[]{:S(2)}) collective-permute-start(bf16[1856,128]{1,0:T(8,128)(2,1)S(1)} %all_gather.31.refs_1_), channel_id=1, source_target_pairs={{0,2},{2,4},{4,6},{6,8},{8,10},{10,12},{12,14},{14,0},{1,15},{3,1}... | collective-permute-start | bytes 1425416 | tf_op jit(solution)/shard_map/ppermute | solution.py:280
  37.5 2.1 %collective-permute-start.3 = (bf16[1792,128]{1,0:T(8,128)(2,1)S(1)}, bf16[1792,128]{1,0:T(8,128)(2,1)S(1)}, u32[]{:S(2)}, u32[]{:S(2)}) collective-permute-start(bf16[1792,128]{1,0:T(8,128)(2,1)S(1)} %collective-permute-done.2), channel_id=1, source_target_pairs={{0,2},{2,4},{4,6},{6,8},{8,10},{10,12},{12,14},{14,0},{1,15},{3,1}... | collective-permute-start | bytes 1376264 | tf_op jit(solution)/shard_map/ppermute | solution.py:282
  39.6 2.6 %all_gather.32.refs_2_ = bf16[3584,128]{1,0:T(8,128)(2,1)} all-gather(bf16[1792,128]{1,0:T(8,128)(2,1)S(1)} %collective-permute-done.2), channel_id=1, replica_groups={{0,1},{2,3},{4,5},{6,7},{8,9},{10,11},{12,13},{14,15},{16,17},{18,19},{..., dimensions={0}, use_global_device_ids=true | all-gather | bytes 1376256 | tf_op jit(solution)/shard_map/all_gather | solution.py:260
  42.2 0.0 copy-done
  42.2 5.7 %collective-permute-done.3 = bf16[1792,128]{1,0:T(8,128)(2,1)S(1)} collective-permute-done((bf16[1792,128]{1,0:T(8,128)(2,1)S(1)}, bf16[1792,128]{1,0:T(8,128)(2,1)S(1)}, u32[]{:S(2)}, u32[]{:S(2)}) %collective-permute-start.3) | collective-permute-done | bytes 458784 | tf_op jit(solution)/shard_map/ppermute | solution.py:282
  48.0 5.0 %collective-permute-start.4 = (bf16[1792,128]{1,0:T(8,128)(2,1)S(1)}, bf16[1792,128]{1,0:T(8,128)(2,1)S(1)}, u32[]{:S(2)}, u32[]{:S(2)}) collective-permute-start(bf16[1792,128]{1,0:T(8,128)(2,1)S(1)} %collective-permute-done.3), channel_id=1, source_target_pairs={{0,2},{2,4},{4,6},{6,8},{8,10},{10,12},{12,14},{14,0},{1,15},{3,1}... | collective-permute-start | bytes 1376264 | tf_op jit(solution)/shard_map/ppermute | solution.py:282
  53.0 0.0 collective-permute-done.5
  53.0 1.9 %collective-permute-start.6 = (bf16[1856,128]{1,0:T(8,128)(2,1)S(1)}, bf16[1856,128]{1,0:T(8,128)(2,1)S(1)}, u32[]{:S(2)}, u32[]{:S(2)}) collective-permute-start(bf16[1856,128]{1,0:T(8,128)(2,1)S(1)} %collective-permute-done.5), channel_id=1, source_target_pairs={{0,2},{2,4},{4,6},{6,8},{8,10},{10,12},{12,14},{14,0},{1,15},{3,1}... | collective-permute-start | bytes 1425416 | tf_op jit(solution)/shard_map/ppermute | solution.py:283
  54.9 2.6 %all_gather.33.refs_3_ = bf16[3584,128]{1,0:T(8,128)(2,1)} all-gather(bf16[1792,128]{1,0:T(8,128)(2,1)S(1)} %collective-permute-done.3), channel_id=1, replica_groups={{0,1},{2,3},{4,5},{6,7},{8,9},{10,11},{12,13},{14,15},{16,17},{18,19},{..., dimensions={0}, use_global_device_ids=true | all-gather | bytes 1376256 | tf_op jit(solution)/shard_map/all_gather | solution.py:260
  57.5 2.6 %all_gather.35.refs_5_ = bf16[3712,128]{1,0:T(8,128)(2,1)} all-gather(bf16[1856,128]{1,0:T(8,128)(2,1)S(1)} %collective-permute-done.5), channel_id=1, replica_groups={{0,1},{2,3},{4,5},{6,7},{8,9},{10,11},{12,13},{14,15},{16,17},{18,19},{..., dimensions={0}, use_global_device_ids=true | all-gather | bytes 1425408 | tf_op jit(solution)/shard_map/all_gather | solution.py:260
  60.1 0.0 collective-permute-done.4
  60.2 3.3 %collective-permute-start.8 = (bf16[896,128]{1,0:T(8,128)(2,1)S(1)}, bf16[896,128]{1,0:T(8,128)(2,1)S(1)}, u32[]{:S(2)}, u32[]{:S(2)}) collective-permute-start(bf16[896,128]{1,0:T(8,128)(2,1)S(1)} %constant_dynamic-slice_fusion.1), channel_id=1, source_target_pairs={{0,2},{2,4},{4,6},{6,8},{8,10},{10,12},{12,14},{14,0},{1,15},{3,1}... | collective-permute-start | bytes 688136 | tf_op jit(solution)/shard_map/ppermute | solution.py:284
  63.5 0.0 collective-permute-done.6
  63.5 5.0 %collective-permute-start.7 = (bf16[1856,128]{1,0:T(8,128)(2,1)S(1)}, bf16[1856,128]{1,0:T(8,128)(2,1)S(1)}, u32[]{:S(2)}, u32[]{:S(2)}) collective-permute-start(bf16[1856,128]{1,0:T(8,128)(2,1)S(1)} %collective-permute-done.6), channel_id=1, source_target_pairs={{0,2},{2,4},{4,6},{6,8},{8,10},{10,12},{12,14},{14,0},{1,15},{3,1}... | collective-permute-start | bytes 1425416 | tf_op jit(solution)/shard_map/ppermute | solution.py:283
  68.5 2.6 %all_gather.34.refs_4_ = bf16[3584,128]{1,0:T(8,128)(2,1)} all-gather(bf16[1792,128]{1,0:T(8,128)(2,1)S(1)} %collective-permute-done.4), channel_id=1, replica_groups={{0,1},{2,3},{4,5},{6,7},{8,9},{10,11},{12,13},{14,15},{16,17},{18,19},{..., dimensions={0}, use_global_device_ids=true | all-gather | bytes 1376256 | tf_op jit(solution)/shard_map/all_gather | solution.py:260
  71.1 2.6 %all_gather.36.refs_6_ = bf16[3712,128]{1,0:T(8,128)(2,1)} all-gather(bf16[1856,128]{1,0:T(8,128)(2,1)S(1)} %collective-permute-done.6), channel_id=1, replica_groups={{0,1},{2,3},{4,5},{6,7},{8,9},{10,11},{12,13},{14,15},{16,17},{18,19},{..., dimensions={0}, use_global_device_ids=true | all-gather | bytes 1425408 | tf_op jit(solution)/shard_map/all_gather | solution.py:260
  73.7 0.0 collective-permute-done.8
  73.7 2.3 %all_gather.38.refs_8_ = bf16[1792,128]{1,0:T(8,128)(2,1)} all-gather(bf16[896,128]{1,0:T(8,128)(2,1)S(1)} %collective-permute-done.8), channel_id=1, replica_groups={{0,1},{2,3},{4,5},{6,7},{8,9},{10,11},{12,13},{14,15},{16,17},{18,19},{..., dimensions={0}, use_global_device_ids=true | all-gather | bytes 688128 | tf_op jit(solution)/shard_map/all_gather | solution.py:260
  76.0 0.0 collective-permute-done.7
  76.0 4.5 %collective-permute-start.9 = (bf16[928,128]{1,0:T(8,128)(2,1)S(1)}, bf16[928,128]{1,0:T(8,128)(2,1)S(1)}, u32[]{:S(2)}, u32[]{:S(2)}) collective-permute-start(bf16[928,128]{1,0:T(8,128)(2,1)S(1)} %constant_dynamic-slice_fusion), channel_id=1, source_target_pairs={{0,2},{2,4},{4,6},{6,8},{8,10},{10,12},{12,14},{14,0},{1,15},{3,1}... | collective-permute-start | bytes 712712 | tf_op jit(solution)/shard_map/ppermute | solution.py:285
  80.5 2.6 %all_gather.37.refs_7_ = bf16[3712,128]{1,0:T(8,128)(2,1)} all-gather(bf16[1856,128]{1,0:T(8,128)(2,1)S(1)} %collective-permute-done.7), channel_id=1, replica_groups={{0,1},{2,3},{4,5},{6,7},{8,9},{10,11},{12,13},{14,15},{16,17},{18,19},{..., dimensions={0}, use_global_device_ids=true | all-gather | bytes 1425408 | tf_op jit(solution)/shard_map/all_gather | solution.py:260
  83.1 0.4 collective-permute-done.9
  83.5 6.0 %all_gather.39.refs_9_ = bf16[1856,128]{1,0:T(8,128)(2,1)} all-gather(bf16[928,128]{1,0:T(8,128)(2,1)S(1)} %collective-permute-done.9), channel_id=1, replica_groups={{0,1},{2,3},{4,5},{6,7},{8,9},{10,11},{12,13},{14,15},{16,17},{18,19},{..., dimensions={0}, use_global_device_ids=true | all-gather | bytes 712704 | tf_op jit(solution)/shard_map/all_gather | solution.py:260
  89.5 19.4 %multiply.1 = bf16[24,128,128]{2,1,0:T(8,128)(2,1)} custom-call(s32[2,12]{1,0:T(2,128)} %bitcast.9, bf16[1792,128]{1,0:T(8,128)(2,1)} %copy-done.1, bf16[1856,128]{1,0:T(8,128)(2,1)} %copy-done, bf16[3584,128]{1,0:T(8,128)(2,1)} %all_gather.32.refs_2_, bf16[3584,128]{1,0:T(8,128)(2,1)} %all_gather.33.refs_3_, bf16[3584,128]{1,0:T(8,128)(2,1)} %all_gather.34.refs_4_, ...), custom_call_target="tpu_custom_call" | custom-call | tf_op jit(solution)/shard_map/multiply/pallas_call | solution.py:289
  (3 shorter events, 0.0 us)
Async XLA Ops:
  10.8 19.5 %copy-start.1 = (bf16[1792,128]{1,0:T(8,128)(2,1)}, bf16[1792,128]{1,0:T(8,128)(2,1)S(1)}, u32[]{:S(2)}) copy-start(bf16[1792,128]{1,0:T(8,128)(2,1)S(1)} %all_gather.30.refs_0_) | copy-start | bytes 1376260
  10.8 20.2 %collective-permute-start.2 = (bf16[1792,128]{1,0:T(8,128)(2,1)S(1)}, bf16[1792,128]{1,0:T(8,128)(2,1)S(1)}, u32[]{:S(2)}, u32[]{:S(2)}) collective-permute-start(bf16[1792,128]{1,0:T(8,128)(2,1)S(1)} %all_gather.30.refs_0_), channel_id=1, source_target_pairs={{0,2},{2,4},{4,6},{6,8},{8,10},{10,12},{12,14},{14,0},{1,15},{3,1}... | collective-permute-start | bytes 1376264 | tf_op jit(solution)/shard_map/ppermute | solution.py:275
  18.1 10.5 %collective-permute-start = (bf16[768,128]{1,0:T(8,128)(2,1)}, bf16[768,128]{1,0:T(8,128)(2,1)S(1)}, u32[]{:S(2)}, u32[]{:S(2)}) collective-permute-start(bf16[768,128]{1,0:T(8,128)(2,1)} %get-tuple-element.18), channel_id=1, source_target_pairs={{0,16},{16,32},{32,48},{48,64},{64,80},{80,96},{96,112},{112,128},... | collective-permute-start | bytes 589832 | tf_op jit(solution)/shard_map/ppermute | solution.py:276
  21.2 9.1 %copy-start.2 = (bf16[128,128]{1,0:T(8,128)(2,1)S(1)}, bf16[128,128]{1,0:T(8,128)(2,1)}, u32[]{:S(2)}) copy-start(bf16[128,128]{1,0:T(8,128)(2,1)} %get-tuple-element.16) | copy-start | bytes 98308
  21.3 9.0 %collective-permute-start.1 = (bf16[768,128]{1,0:T(8,128)(2,1)}, bf16[768,128]{1,0:T(8,128)(2,1)S(1)}, u32[]{:S(2)}, u32[]{:S(2)}) collective-permute-start(bf16[768,128]{1,0:T(8,128)(2,1)} %get-tuple-element.19), channel_id=1, source_target_pairs={{16,0},{32,16},{48,32},{64,48},{80,64},{96,80},{112,96},{128,112},... | collective-permute-start | bytes 589832 | tf_op jit(solution)/shard_map/ppermute | solution.py:276
  30.3 0.7 copy-start.3
  33.1 9.1 %copy-start = (bf16[1856,128]{1,0:T(8,128)(2,1)}, bf16[1856,128]{1,0:T(8,128)(2,1)S(1)}, u32[]{:S(2)}) copy-start(bf16[1856,128]{1,0:T(8,128)(2,1)S(1)} %all_gather.31.refs_1_) | copy-start | bytes 1425412
  33.1 19.9 %collective-permute-start.5 = (bf16[1856,128]{1,0:T(8,128)(2,1)S(1)}, bf16[1856,128]{1,0:T(8,128)(2,1)S(1)}, u32[]{:S(2)}, u32[]{:S(2)}) collective-permute-start(bf16[1856,128]{1,0:T(8,128)(2,1)S(1)} %all_gather.31.refs_1_), channel_id=1, source_target_pairs={{0,2},{2,4},{4,6},{6,8},{8,10},{10,12},{12,14},{14,0},{1,15},{3,1}... | collective-permute-start | bytes 1425416 | tf_op jit(solution)/shard_map/ppermute | solution.py:280
  37.5 10.5 %collective-permute-start.3 = (bf16[1792,128]{1,0:T(8,128)(2,1)S(1)}, bf16[1792,128]{1,0:T(8,128)(2,1)S(1)}, u32[]{:S(2)}, u32[]{:S(2)}) collective-permute-start(bf16[1792,128]{1,0:T(8,128)(2,1)S(1)} %collective-permute-done.2), channel_id=1, source_target_pairs={{0,2},{2,4},{4,6},{6,8},{8,10},{10,12},{12,14},{14,0},{1,15},{3,1}... | collective-permute-start | bytes 1376264 | tf_op jit(solution)/shard_map/ppermute | solution.py:282
  48.0 12.2 %collective-permute-start.4 = (bf16[1792,128]{1,0:T(8,128)(2,1)S(1)}, bf16[1792,128]{1,0:T(8,128)(2,1)S(1)}, u32[]{:S(2)}, u32[]{:S(2)}) collective-permute-start(bf16[1792,128]{1,0:T(8,128)(2,1)S(1)} %collective-permute-done.3), channel_id=1, source_target_pairs={{0,2},{2,4},{4,6},{6,8},{8,10},{10,12},{12,14},{14,0},{1,15},{3,1}... | collective-permute-start | bytes 1376264 | tf_op jit(solution)/shard_map/ppermute | solution.py:282
  53.0 10.5 %collective-permute-start.6 = (bf16[1856,128]{1,0:T(8,128)(2,1)S(1)}, bf16[1856,128]{1,0:T(8,128)(2,1)S(1)}, u32[]{:S(2)}, u32[]{:S(2)}) collective-permute-start(bf16[1856,128]{1,0:T(8,128)(2,1)S(1)} %collective-permute-done.5), channel_id=1, source_target_pairs={{0,2},{2,4},{4,6},{6,8},{8,10},{10,12},{12,14},{14,0},{1,15},{3,1}... | collective-permute-start | bytes 1425416 | tf_op jit(solution)/shard_map/ppermute | solution.py:283
  60.2 13.6 %collective-permute-start.8 = (bf16[896,128]{1,0:T(8,128)(2,1)S(1)}, bf16[896,128]{1,0:T(8,128)(2,1)S(1)}, u32[]{:S(2)}, u32[]{:S(2)}) collective-permute-start(bf16[896,128]{1,0:T(8,128)(2,1)S(1)} %constant_dynamic-slice_fusion.1), channel_id=1, source_target_pairs={{0,2},{2,4},{4,6},{6,8},{8,10},{10,12},{12,14},{14,0},{1,15},{3,1}... | collective-permute-start | bytes 688136 | tf_op jit(solution)/shard_map/ppermute | solution.py:284
  63.5 12.4 %collective-permute-start.7 = (bf16[1856,128]{1,0:T(8,128)(2,1)S(1)}, bf16[1856,128]{1,0:T(8,128)(2,1)S(1)}, u32[]{:S(2)}, u32[]{:S(2)}) collective-permute-start(bf16[1856,128]{1,0:T(8,128)(2,1)S(1)} %collective-permute-done.6), channel_id=1, source_target_pairs={{0,2},{2,4},{4,6},{6,8},{8,10},{10,12},{12,14},{14,0},{1,15},{3,1}... | collective-permute-start | bytes 1425416 | tf_op jit(solution)/shard_map/ppermute | solution.py:283
  76.0 7.5 %collective-permute-start.9 = (bf16[928,128]{1,0:T(8,128)(2,1)S(1)}, bf16[928,128]{1,0:T(8,128)(2,1)S(1)}, u32[]{:S(2)}, u32[]{:S(2)}) collective-permute-start(bf16[928,128]{1,0:T(8,128)(2,1)S(1)} %constant_dynamic-slice_fusion), channel_id=1, source_target_pairs={{0,2},{2,4},{4,6},{6,8},{8,10},{10,12},{12,14},{14,0},{1,15},{3,1}... | collective-permute-start | bytes 712712 | tf_op jit(solution)/shard_map/ppermute | solution.py:285
